TPU v7x, 32 devices: a whole 2x2x4 slice. The times are simulated.
32 devices in a mesh: dp: 4 (over x, core), seq: 8 (over z, y).
Axes of the slice: x: 2, y: 2, z: 4, core: 2. Of those that a mesh axis runs over, the one named last changes fastest.
Arguments:
- frames: bfloat16 [4, 1024, 1024], P('dp', 'seq'), may hold values from -6 to 6
- skip: bfloat16 [4, 1024, 1024], P('dp', 'seq'), may hold values from -6 to 6
- lengths: int32 [4, 8], P('dp'), may hold values from 1 to 897, 1024 in all within a row
- frame_mask: int32 [4, 1024], P('dp', 'seq'), may hold values 0 or 1
- time_step: int32 [4, 8], P('dp'), may hold values from 0 to 31
- w_skip: bfloat16 [2048, 1024], replicated, may hold values from -0.125 to 0.125
- w_ada: bfloat16 [1024, 2048], replicated, may hold values from -0.1875 to 0.1875
- b_ada: bfloat16 [2048], replicated, may hold values from -4 to 4
- w_qkv: bfloat16 [1024, 3072], replicated, may hold values from -0.1875 to 0.1875
- w_out: bfloat16 [1024, 1024], replicated, may hold values from -0.5 to 0.5
- norm_gain: bfloat16 [1024], replicated, may hold values from 0.25 to 1.75
- w_up: bfloat16 [1024, 4096], replicated, may hold values from -0.1875 to 0.1875
- b_up: bfloat16 [4096], replicated, may hold values from -6 to 6
- w_down: bfloat16 [4096, 1024], replicated, may hold values from -0.09375 to 0.09375
- b_down: bfloat16 [1024], replicated, may hold values from -4 to 4
- cotangent: bfloat16 [4, 1024, 1024], P('dp', 'seq'), may hold values from -6 to 6
Outputs:
- result: bfloat16 [4, 1024, 1024], P('dp', 'seq')
- grad_frames: float32 [4, 1024, 1024], P('dp', 'seq')
- grad_skip_in: float32 [4, 1024, 1024], P('dp', 'seq')
- grad_w_skip: float32 [2048, 1024], P('seq')
- grad_w_ada: float32 [1024, 2048], P('seq')
- grad_b_ada: float32 [2048], P('seq')
- grad_w_qkv: float32 [1024, 3072], P('seq')
- grad_w_out: float32 [1024, 1024], P('seq')
- grad_gain: float32 [1024], P('seq')
- grad_w_up: float32 [1024, 4096], P('seq')
- grad_b_up: float32 [4096], P('seq')
- grad_w_down: float32 [4096, 1024], P('seq')
- grad_b_down: float32 [1024], P('seq')
Inputs may be any that keep to these rules, and one draw needn't show every extreme that they name: In each row the 8 lengths sum to 1024, and the longest is exactly 897.
All inputs are finite; a program needn't handle non-finite values. No bound on the sum of `frame_mask` on one device may be relied on, other than what follows from the above.
Results may differ from a plain program's by a relative error of at most 0.02.
Values may be sent and summed in bfloat16 or wider, within the bound.
A program may use at most 320 MiB of HBM per device.

v0:
```python
import math

import jax
import jax.numpy as jnp
from jax import lax
from jax.sharding import PartitionSpec as P

HEADS = 16
HEAD = 64
TSTEPS = 32


precise = lax.Precision.HIGHEST
masked_score = -1e30
contract_rows = (((0,), (0,)), ((), ()))
contract_cols = (((1,), (1,)), ((), ()))


def divisor_below(count_all, upper_limit):
    size_now = min(count_all, upper_limit)
    while count_all % size_now:
        size_now -= 1
    return size_now


def normalize(values):
    centered = values - jnp.mean(values, axis=-1, keepdims=True)
    variance = jnp.mean(centered * centered, axis=-1, keepdims=True)
    return centered * lax.rsqrt(variance + 1e-06)


def segment_of(lengths, frame_index):
    utter_ends = jnp.cumsum(lengths)
    return jnp.sum((frame_index[:, None] >= utter_ends[None, :]).astype(jnp.int32), axis=1)


def utterance_layout(lengths, frame_index):
    utter_ends = jnp.cumsum(lengths)
    starts = utter_ends - lengths
    segment = segment_of(lengths, frame_index)
    member = segment[:, None] == jnp.arange(lengths.shape[0], dtype=jnp.int32)[None, :]
    position = frame_index - jnp.sum(jnp.where(member, starts[None, :], 0), axis=1)
    return (segment, position, member)


def rotary_tables(position, head_size):
    half_size = head_size // 2
    frequency = jnp.exp(
        jnp.arange(half_size, dtype=jnp.float32) * (-2.0 * math.log(10000.0) / head_size)
    )
    angles = position.astype(jnp.float32)[:, None] * frequency[None, :]
    return (jnp.cos(angles)[:, None, :], jnp.sin(angles)[:, None, :])


def rotate(values, cos_table, sin_table):
    half_size = values.shape[-1] // 2
    first_half = values[..., :half_size]
    second_half = values[..., half_size:]
    return jnp.concatenate(
        [
            first_half * cos_table - second_half * sin_table,
            second_half * cos_table + first_half * sin_table,
        ],
        axis=-1,
    )


def rotate_back(values, cos_table, sin_table):
    half_size = values.shape[-1] // 2
    first_half = values[..., :half_size]
    second_half = values[..., half_size:]
    return jnp.concatenate(
        [
            first_half * cos_table + second_half * sin_table,
            second_half * cos_table - first_half * sin_table,
        ],
        axis=-1,
    )


def time_embedding(steps, model_width):
    half_size = model_width // 2
    flow_time = steps.astype(jnp.float32) / TSTEPS
    frequency = jnp.exp(jnp.arange(half_size, dtype=jnp.float32) * (-math.log(10000.0) / half_size))
    angles = 1000.0 * flow_time[:, None] * frequency[None, :]
    return jnp.concatenate([jnp.sin(angles), jnp.cos(angles)], axis=1)


def make_attend(query_low, query_segment, query_index, lengths):
    count_rows, head_count, head_size = query_low.shape
    scale_factor = 1.0 / math.sqrt(head_size)

    def attend(running, key_piece, first_row):
        keys_part, values_part, valid_part = key_piece
        count_keys = keys_part.shape[0]
        block_rows = divisor_below(count_keys, 1024)
        block_count = count_keys // block_rows
        key_blocks = keys_part.reshape(block_count, block_rows, head_count, head_size)
        value_blocks = values_part.reshape(block_count, block_rows, head_count, head_size)
        valid_blocks = valid_part.reshape(block_count, block_rows)
        offsets = first_row + jnp.arange(block_count, dtype=jnp.int32) * block_rows

        def attend_block_step(carried, inputs):
            row_top, row_total, weighted = carried
            key_block, value_block, valid_block, offset = inputs
            key_index = offset + jnp.arange(block_rows, dtype=jnp.int32)
            key_segment = segment_of(lengths, key_index)
            allowed = (query_segment[:, None] == key_segment[None, :]) & (
                (valid_block[None, :] > 0) | (query_index[:, None] == key_index[None, :])
            )
            scores = (
                jnp.einsum("qhd,khd->hqk", query_low, key_block, preferred_element_type=jnp.float32)
                * scale_factor
            )
            scores = jnp.where(allowed[None], scores, masked_score)
            new_top = jnp.maximum(row_top, jnp.max(scores, axis=2))
            weights = jnp.where(allowed[None], jnp.exp(scores - new_top[:, :, None]), 0.0)
            factor = jnp.exp(row_top - new_top)
            row_total = row_total * factor + jnp.sum(weights, axis=2)
            weighted = weighted * jnp.transpose(factor)[:, :, None] + jnp.einsum(
                "hqk,khd->qhd",
                weights.astype(jnp.bfloat16),
                value_block,
                preferred_element_type=jnp.float32,
            )
            return ((new_top, row_total, weighted), None)

        result_state, unused = lax.scan(
            attend_block_step, running, (key_blocks, value_blocks, valid_blocks, offsets)
        )
        return result_state

    return attend


def key_sweep(
    query_low, grad_attn, log_total, row_delta, query_segment, query_index, lengths, key_tuple
):
    keys_all, values_all, valid_all = key_tuple
    count_rows, head_count, head_size = query_low.shape
    scale_factor = 1.0 / math.sqrt(head_size)
    count_keys = keys_all.shape[0]
    block_rows = divisor_below(count_keys, 1024)
    block_count = count_keys // block_rows
    key_blocks = keys_all.reshape(block_count, block_rows, head_count, head_size)
    value_blocks = values_all.reshape(block_count, block_rows, head_count, head_size)
    valid_blocks = valid_all.reshape(block_count, block_rows)
    offsets = jnp.arange(block_count, dtype=jnp.int32) * block_rows
    top_shift = jnp.transpose(log_total)[:, :, None]
    delta_shift = jnp.transpose(row_delta)[:, :, None]

    def key_block_step(grad_query, inputs):
        key_block, value_block, valid_block, offset = inputs
        key_index = offset + jnp.arange(block_rows, dtype=jnp.int32)
        key_segment = segment_of(lengths, key_index)
        allowed = (query_segment[:, None] == key_segment[None, :]) & (
            (valid_block[None, :] > 0) | (query_index[:, None] == key_index[None, :])
        )
        scores = (
            jnp.einsum("qhd,khd->hqk", query_low, key_block, preferred_element_type=jnp.float32)
            * scale_factor
        )
        weights = jnp.where(allowed[None], jnp.exp(scores - top_shift), 0.0)
        grad_weights = jnp.einsum(
            "qhd,khd->hqk", grad_attn, value_block, preferred_element_type=jnp.float32
        )
        grad_scores = (weights * (grad_weights - delta_shift)).astype(jnp.bfloat16)
        grad_query = (
            grad_query
            + jnp.einsum("hqk,khd->qhd", grad_scores, key_block, preferred_element_type=jnp.float32)
            * scale_factor
        )
        grad_key = (
            jnp.einsum("hqk,qhd->khd", grad_scores, query_low, preferred_element_type=jnp.float32)
            * scale_factor
        )
        grad_value = jnp.einsum(
            "hqk,qhd->khd",
            weights.astype(jnp.bfloat16),
            grad_attn,
            preferred_element_type=jnp.float32,
        )
        return (grad_query, (grad_key, grad_value))

    start_grad = jnp.zeros((count_rows, head_count, head_size), jnp.float32)
    return lax.scan(key_block_step, start_grad, (key_blocks, value_blocks, valid_blocks, offsets))


def on_device(
    frames,
    skip,
    lengths,
    frame_mask,
    time_step,
    w_skip,
    w_ada,
    b_ada,
    w_qkv,
    w_out,
    norm_gain,
    w_up,
    b_up,
    w_down,
    b_down,
    cotangent,
):
    local_frames = frames[0]
    local_skip = skip[0]
    row_lengths = lengths[0]
    count_rows, model_width = local_frames.shape
    head_count = HEADS
    head_size = HEAD
    row_base = lax.axis_index("seq") * count_rows
    frame_index = row_base + jnp.arange(count_rows, dtype=jnp.int32)
    segment, position, member = utterance_layout(row_lengths, frame_index)
    member_float = member.astype(jnp.float32)
    embed_low = time_embedding(time_step[0], model_width).astype(jnp.bfloat16)
    ada_table = jnp.dot(embed_low, w_ada, preferred_element_type=jnp.float32) + b_ada.astype(
        jnp.float32
    )
    ada_frame = jnp.dot(member_float, ada_table, precision=precise)
    scale_part = ada_frame[:, :model_width]
    shift_part = ada_frame[:, model_width:]
    joined = jnp.concatenate([local_frames, local_skip], axis=1)
    residual_in = jnp.dot(joined, w_skip, preferred_element_type=jnp.float32)
    norm_first, first_pull = jax.vjp(normalize, residual_in)
    first_low = (norm_first * (1.0 + scale_part) + shift_part).astype(jnp.bfloat16)
    packed = jnp.dot(first_low, w_qkv, preferred_element_type=jnp.float32)
    cos_table, sin_table = rotary_tables(position, head_size)
    query_low = rotate(
        packed[:, :model_width].reshape(count_rows, head_count, head_size), cos_table, sin_table
    ).astype(jnp.bfloat16)
    keys_low = (
        rotate(
            packed[:, model_width : 2 * model_width].reshape(count_rows, head_count, head_size),
            cos_table,
            sin_table,
        )
        .astype(jnp.bfloat16)
        .reshape(count_rows, model_width)
    )
    values_low = packed[:, 2 * model_width :].astype(jnp.bfloat16)
    valid_low = frame_mask[0].astype(jnp.bfloat16)
    attend = make_attend(query_low, segment, frame_index, row_lengths)
    start_state = (
        jnp.full((head_count, count_rows), masked_score, jnp.float32),
        jnp.zeros((head_count, count_rows), jnp.float32),
        jnp.zeros((count_rows, head_count, head_size), jnp.float32),
    )
    gathered = (
        lax.all_gather(keys_low, "seq", axis=0, tiled=True),
        lax.all_gather(values_low, "seq", axis=0, tiled=True),
        lax.all_gather(valid_low, "seq", axis=0, tiled=True),
    )
    row_top, row_total, weighted = attend(start_state, gathered, 0)
    attn_sum = weighted / jnp.transpose(row_total)[:, :, None]
    log_total = jnp.transpose(row_top + jnp.log(row_total))
    attn_low = attn_sum.reshape(count_rows, model_width).astype(jnp.bfloat16)
    residual_mid = residual_in + jnp.dot(attn_low, w_out, preferred_element_type=jnp.float32)
    gain_float = norm_gain.astype(jnp.float32)
    second_float, second_pull = jax.vjp(
        lambda hidden, gain_vector: normalize(hidden) * gain_vector, residual_mid, gain_float
    )
    second_low = second_float.astype(jnp.bfloat16)
    upper_sum = jnp.dot(second_low, w_up, preferred_element_type=jnp.float32) + b_up.astype(
        jnp.float32
    )
    gated_float, gelu_pull = jax.vjp(
        lambda hidden: jax.nn.gelu(hidden, approximate=True), upper_sum
    )
    gated_low = gated_float.astype(jnp.bfloat16)
    output = (
        residual_mid
        + jnp.dot(gated_low, w_down, preferred_element_type=jnp.float32)
        + b_down.astype(jnp.float32)
    )
    grad_out = cotangent[0]
    grad_out_float = grad_out.astype(jnp.float32)
    grad_down = lax.dot_general(
        gated_low, grad_out, contract_rows, preferred_element_type=jnp.float32
    )
    grad_down_bias = jnp.sum(grad_out_float, axis=0)
    grad_gated = lax.dot_general(
        grad_out, w_down, contract_cols, preferred_element_type=jnp.float32
    )
    grad_upper = gelu_pull(grad_gated)[0].astype(jnp.bfloat16)
    grad_up = lax.dot_general(
        second_low, grad_upper, contract_rows, preferred_element_type=jnp.float32
    )
    grad_up_bias = jnp.sum(grad_upper.astype(jnp.float32), axis=0)
    grad_second = lax.dot_general(
        grad_upper, w_up, contract_cols, preferred_element_type=jnp.float32
    )
    grad_mid_norm, grad_gain = second_pull(grad_second)
    grad_mid = grad_out_float + grad_mid_norm
    grad_branch = grad_mid.astype(jnp.bfloat16)
    grad_out_weight = lax.dot_general(
        attn_low, grad_branch, contract_rows, preferred_element_type=jnp.float32
    )
    grad_attn = (
        lax.dot_general(grad_branch, w_out, contract_cols, preferred_element_type=jnp.float32)
        .astype(jnp.bfloat16)
        .reshape(count_rows, head_count, head_size)
    )
    row_delta = jnp.sum(grad_attn.astype(jnp.float32) * attn_sum, axis=2)
    grad_query, key_parts = key_sweep(
        query_low, grad_attn, log_total, row_delta, segment, frame_index, row_lengths, gathered
    )
    grad_key_all, grad_value_all = key_parts
    total_keys = grad_key_all.shape[0] * grad_key_all.shape[1]
    grad_key, grad_value = (
        lax.psum_scatter(
            grad_key_all.reshape(total_keys, model_width), "seq", scatter_dimension=0, tiled=True
        ),
        lax.psum_scatter(
            grad_value_all.reshape(total_keys, model_width), "seq", scatter_dimension=0, tiled=True
        ),
    )
    grad_key = rotate_back(
        grad_key.reshape(count_rows, head_count, head_size), cos_table, sin_table
    ).reshape(count_rows, model_width)
    grad_query = rotate_back(grad_query, cos_table, sin_table).reshape(count_rows, model_width)
    grad_packed = jnp.concatenate([grad_query, grad_key, grad_value], axis=1).astype(jnp.bfloat16)
    grad_qkv = lax.dot_general(
        first_low, grad_packed, contract_rows, preferred_element_type=jnp.float32
    )
    grad_first = lax.dot_general(
        grad_packed, w_qkv, contract_cols, preferred_element_type=jnp.float32
    )
    grad_ada_frame = jnp.concatenate([grad_first * norm_first, grad_first], axis=1)
    grad_ada_table = lax.dot_general(member_float, grad_ada_frame, contract_rows, precision=precise)
    grad_ada = lax.dot_general(
        embed_low.astype(jnp.float32), grad_ada_table, contract_rows, precision=precise
    )
    grad_ada_bias = jnp.sum(grad_ada_table, axis=0)
    grad_in = (grad_mid + first_pull(grad_first * (1.0 + scale_part))[0]).astype(jnp.bfloat16)
    grad_skip_weight = lax.dot_general(
        joined, grad_in, contract_rows, preferred_element_type=jnp.float32
    )
    grad_joined = lax.dot_general(
        grad_in, w_skip, contract_cols, preferred_element_type=jnp.float32
    )
    (
        share_skip,
        share_ada,
        share_ada_bias,
        share_qkv,
        share_out,
        share_gain,
        share_up,
        share_up_bias,
        share_down,
        share_down_bias,
    ) = (
        lax.psum_scatter(grad_skip_weight, "seq", scatter_dimension=0, tiled=True),
        lax.psum_scatter(grad_ada, "seq", scatter_dimension=0, tiled=True),
        lax.psum_scatter(grad_ada_bias, "seq", scatter_dimension=0, tiled=True),
        lax.psum_scatter(grad_qkv, "seq", scatter_dimension=0, tiled=True),
        lax.psum_scatter(grad_out_weight, "seq", scatter_dimension=0, tiled=True),
        lax.psum_scatter(grad_gain, "seq", scatter_dimension=0, tiled=True),
        lax.psum_scatter(grad_up, "seq", scatter_dimension=0, tiled=True),
        lax.psum_scatter(grad_up_bias, "seq", scatter_dimension=0, tiled=True),
        lax.psum_scatter(grad_down, "seq", scatter_dimension=0, tiled=True),
        lax.psum_scatter(grad_down_bias, "seq", scatter_dimension=0, tiled=True),
    )
    (
        total_skip,
        total_ada,
        total_ada_bias,
        total_qkv,
        total_out,
        total_gain,
        total_up,
        total_up_bias,
        total_down,
        total_down_bias,
    ) = (
        lax.psum(share_skip.astype(jnp.bfloat16), "dp").astype(jnp.float32),
        lax.psum(share_ada.astype(jnp.bfloat16), "dp").astype(jnp.float32),
        lax.psum(share_ada_bias.astype(jnp.bfloat16), "dp").astype(jnp.float32),
        lax.psum(share_qkv.astype(jnp.bfloat16), "dp").astype(jnp.float32),
        lax.psum(share_out.astype(jnp.bfloat16), "dp").astype(jnp.float32),
        lax.psum(share_gain.astype(jnp.bfloat16), "dp").astype(jnp.float32),
        lax.psum(share_up.astype(jnp.bfloat16), "dp").astype(jnp.float32),
        lax.psum(share_up_bias.astype(jnp.bfloat16), "dp").astype(jnp.float32),
        lax.psum(share_down.astype(jnp.bfloat16), "dp").astype(jnp.float32),
        lax.psum(share_down_bias.astype(jnp.bfloat16), "dp").astype(jnp.float32),
    )
    return (
        output.astype(jnp.bfloat16)[None],
        grad_joined[:, :model_width][None],
        grad_joined[:, model_width:][None],
        total_skip,
        total_ada,
        total_ada_bias,
        total_qkv,
        total_out,
        total_gain,
        total_up,
        total_up_bias,
        total_down,
        total_down_bias,
    )


def solution(mesh):
    placed = (
        P("dp", "seq", None),
        P("dp", "seq", None),
        P("dp", None),
        P("dp", "seq"),
        P("dp", None),
        P(),
        P(),
        P(),
        P(),
        P(),
        P(),
        P(),
        P(),
        P(),
        P(),
        P("dp", "seq", None),
    )
    return jax.shard_map(
        on_device,
        mesh=mesh,
        in_specs=placed,
        out_specs=(
            P("dp", "seq", None),
            P("dp", "seq", None),
            P("dp", "seq", None),
            P("seq", None),
            P("seq", None),
            P("seq"),
            P("seq", None),
            P("seq", None),
            P("seq"),
            P("seq", None),
            P("seq"),
            P("seq", None),
            P("seq"),
        ),
        check_vma=False,
    )
```

profile of v0, /device:TPU:0, one launch (start us, length us, event | category | flops | bytes accessed | tf_op | source)
XLA Modules:
  0.0 1630.7 jit_solution(9915678851859075477)
XLA Ops:
  8.8 3.2 fusion.80
  12.9 3.1 convolution_add_fusion.1
  22.3 2.0 copy.45
  24.5 1.9 subtract_convert_fusion.3
  27.3 1.8 slice.107
  29.8 22.7 %all-gather = bf16[1,1024]{1,0:T(2,128)(2,1)S(1)} all-gather(bf16[1,128]{1,0:T(2,128)(2,1)S(1)} %convert_element_type.166), channel_id=2, replica_groups=mesh['dp'=4,'seq'=8] {'seq'}, dimensions={1}, use_global_device_ids=true | all-gather | bytes 2304 | tf_op jit(solution)/shard_map/all_gather | solution.py:253
  53.5 27.6 %all-gather.4.cloned.1.call-done = bf16[1024,1024]{0,1:T(8,128)(2,1)} async-done(((bf16[128,1024]{0,1:T(8,128)(2,1)}), bf16[1024,1024]{0,1:T(8,128)(2,1)}) %all-gather.4.cloned.1.call-update) | async-done | bytes 2097168 | tf_op jit(solution)/shard_map/all_gather | solution.py:251
  81.1 3.3 select_reduce_fusion
  84.5 2.6 fusion.1
  88.4 42.9 %all-gather.6.cloned.1.call-done = bf16[1024,1024]{1,0:T(8,128)(2,1)} async-done(((bf16[128,1024]{1,0:T(8,128)(2,1)}), bf16[1024,1024]{1,0:T(8,128)(2,1)}) %all-gather.6.cloned.1.call-update) | async-done | bytes 2097168 | tf_op jit(solution)/shard_map/all_gather | solution.py:252
  131.3 3.9 copy.46
  135.3 7.3 fusion.81
  146.5 4.5 convert_reduce_fusion
  151.0 3.5 multiply_reduce_fusion
  159.0 7.3 fusion.3
  167.5 5.8 multiply_convert_fusion
  173.4 3.1 convolution_multiply_fusion
  177.7 2.7 fusion.86
  180.7 4.5 fusion.22
  185.1 68.4 %reduce-scatter.11.cloned.1.call-done = f32[128,1024]{0,1:T(8,128)} async-done(((f32[1024,1024]{0,1:T(8,128)}), f32[128,1024]{0,1:T(8,128)}) %reduce-scatter.11.cloned.1.call-update) | async-done | bytes 524304 | tf_op jit(solution)/shard_map/reduce_scatter | solution.py:315
  253.5 1.8 convert.51
  255.3 90.4 %reduce-scatter.9.cloned.1.call-done = f32[128,1024]{0,1:T(8,128)} async-done(((f32[1024,1024]{0,1:T(8,128)}), f32[128,1024]{0,1:T(8,128)}) %reduce-scatter.9.cloned.1.call-update) | async-done | bytes 524304 | tf_op jit(solution)/shard_map/reduce_scatter | solution.py:312
  347.0 5.4 multiply_reduce_fusion.1
  353.7 4.6 fusion.40
  359.9 5.7 fusion.54
  366.8 8.3 fusion.76
  376.8 8.1 fusion.45
  385.9 7.3 fusion.43
  393.3 43.7 %reduce-scatter.19.cloned.1.call-done = f32[128,1024]{1,0:T(8,128)} async-done(((f32[1024,1024]{1,0:T(8,128)}), f32[128,1024]{1,0:T(8,128)}) %reduce-scatter.19.cloned.1.call-update) | async-done | bytes 524304 | tf_op jit(solution)/shard_map/reduce_scatter | solution.py:359
  437.0 1.8 convert_element_type.198
  438.8 150.9 %reduce-scatter.13.cloned.1.call-done = f32[256,1024]{1,0:T(8,128)} async-done(((f32[2048,1024]{1,0:T(8,128)}), f32[256,1024]{1,0:T(8,128)}) %reduce-scatter.13.cloned.1.call-update) | async-done | bytes 1048592 | tf_op jit(solution)/shard_map/reduce_scatter | solution.py:355
  589.7 2.1 convert_element_type.190
  591.8 149.6 %reduce-scatter.15.cloned.1.call-done = f32[128,2048]{1,0:T(8,128)} async-done(((f32[1024,2048]{1,0:T(8,128)}), f32[128,2048]{1,0:T(8,128)}) %reduce-scatter.15.cloned.1.call-update) | async-done | bytes 1048592 | tf_op jit(solution)/shard_map/reduce_scatter | solution.py:356
  741.3 2.1 convert_element_type.192
  743.4 283.9 %reduce-scatter.21.cloned.1.call-done = f32[128,4096]{1,0:T(8,128)} async-done(((f32[1024,4096]{1,0:T(8,128)}), f32[128,4096]{1,0:T(8,128)}) %reduce-scatter.21.cloned.1.call-update) | async-done | bytes 2097168 | tf_op jit(solution)/shard_map/reduce_scatter | solution.py:361
  1027.3 2.7 convert_element_type.202
  1030.0 282.9 %reduce-scatter.23.cloned.1.call-done = f32[512,1024]{1,0:T(8,128)} async-done(((f32[4096,1024]{1,0:T(8,128)}), f32[512,1024]{1,0:T(8,128)}) %reduce-scatter.23.cloned.1.call-update) | async-done | bytes 2097168 | tf_op jit(solution)/shard_map/reduce_scatter | solution.py:363
  1312.9 2.7 convert_element_type.207
  1315.6 207.6 %reduce-scatter.17.cloned.1.call-done = f32[128,3072]{1,0:T(8,128)} async-done(((f32[1024,3072]{1,0:T(8,128)}), f32[128,3072]{1,0:T(8,128)}) %reduce-scatter.17.cloned.1.call-update) | async-done | bytes 1572880 | tf_op jit(solution)/shard_map/reduce_scatter | solution.py:358
  1523.2 2.4 convert_element_type.196
  1528.2 5.6 fusion.28
  1533.8 35.2 %all-reduce.4 = (bf16[2048]{0:T(1024)(128)(2,1)S(1)}, bf16[1024]{0:T(1024)(128)(2,1)S(1)}, bf16[4096]{0:T(1024)(128)(2,1)S(1)}, bf16[1024]{0:T(1024)(128)(2,1)S(1)}) all-reduce(f32[2048]{0:T(1024)S(1)} %get-tuple-element.144, f32[1024]{0:T(1024)S(1)} %copy-done.43, ...), channel_id=7, replica_groups=mesh['dp'=4,'seq'=8] {'seq'}, use_global_device_ids=true, to_apply=%region_22.23.clone | all-reduce | flops 8192 | bytes 49152
  1569.3 5.6 all-reduce.5
  1577.1 3.9 fusion.85
  1582.1 30.8 %all-reduce.9.cloned.1.call-done = (bf16[256,1024]{1,0:T(8,128)(2,1)}, bf16[128,2048]{1,0:T(8,128)(2,1)}, bf16[128,3072]{1,0:T(8,128)(2,1)}, bf16[128,1024]{1,0:...) async-done(((bf16[256,1024]{1,0:T(8,128)(2,1)}, bf16[128,2048]{1,0:T(8,128)(2,1)}, bf16[128,3072]{1,0:T(8,128)(2,1)}, bf16[128,1024]{1,0:T(8,128)(2,1)}, ...) | async-done | bytes 4194320 | tf_op jit(solution)/shard_map/psum | solution.py:378
  1612.9 2.2 convert_element_type.191
  1615.2 2.2 convert_element_type.193
  1617.4 2.6 convert_element_type.197
  (219 shorter events, 39.6 us)
Async XLA Ops:
  7.2 135.4 %copy-start = (bf16[1024,1024]{1,0:T(8,128)(2,1)S(1)}, bf16[1024,1024]{1,0:T(8,128)(2,1)}, u32[]{:S(2)}) copy-start(bf16[1024,1024]{1,0:T(8,128)(2,1)} %param.25) | copy-start | bytes 6291460
  7.2 5.0 copy-start.59
  7.2 73.9 %all-gather.4.cloned.1.call-start = ((), (), s32[]{:S(2)}) async-start(), calls=%async_computation.8 | async-start | bytes 2359296 | tf_op jit(solution)/shard_map/all_gather | solution.py:251
  7.3 5.1 copy-start.56
  12.0 5.8 copy-start.46
  12.2 5.6 copy-start.50
  12.4 5.4 copy-start.3
  12.8 39.8 %copy-start.48 = (s32[128]{0:T(128)}, s32[128]{0:T(128)S(1)}, u32[]{:S(2)}) copy-start(s32[128]{0:T(128)S(1)} %convert_reduce_fusion.3) | copy-start | bytes 1540
  20.0 9.2 copy-start.60
  20.0 9.2 copy-start.45
  20.0 9.8 copy-start.54
  27.2 104.1 %all-gather.6.cloned.1.call-start = ((), (), s32[]{:S(2)}) async-start(), calls=%async_computation.9 | async-start | bytes 2359296 | tf_op jit(solution)/shard_map/all_gather | solution.py:252
  29.1 224.4 %reduce-scatter.11.cloned.1.call-start = ((), (), s32[]{:S(2)}) async-start(), calls=%async_computation.11 | async-start | bytes 4718592 | tf_op jit(solution)/shard_map/reduce_scatter | solution.py:315
  135.3 8.1 slice-start
  135.3 8.2 slice-start.1
  135.3 8.2 copy-start.39
  143.5 11.0 copy-start.41
  146.5 4.5 copy-start.5
  150.9 3.5 copy-start.12
  166.4 179.3 %reduce-scatter.9.cloned.1.call-start = ((), (), s32[]{:S(2)}) async-start(), calls=%async_computation.10 | async-start | bytes 4718592 | tf_op jit(solution)/shard_map/reduce_scatter | solution.py:312
  167.5 5.8 copy-start.23
  167.5 5.8 copy-start.24
  176.7 260.3 %reduce-scatter.19.cloned.1.call-start = ((), (), s32[]{:S(2)}) async-start(), calls=%async_computation.15 | async-start | bytes 4718592 | tf_op jit(solution)/shard_map/reduce_scatter | solution.py:359
  180.3 165.3 %copy-start.34 = (f32[128,32]{0,1:T(8,128)S(1)}, f32[128,32]{0,1:T(8,128)}, u32[]{:S(2)}) copy-start(f32[128,32]{0,1:T(8,128)} %copy-done.33) | copy-start | bytes 49156
  180.4 165.3 %copy-start.36 = (f32[128,32]{0,1:T(8,128)S(1)}, f32[128,32]{0,1:T(8,128)}, u32[]{:S(2)}) copy-start(f32[128,32]{0,1:T(8,128)} %copy-done.35) | copy-start | bytes 49156
  180.4 166.6 %copy-start.8 = (f32[128,2048]{1,0:T(8,128)S(1)}, f32[128,2048]{1,0:T(8,128)}, u32[]{:S(2)}) copy-start(f32[128,2048]{1,0:T(8,128)} %copy-done.7) | copy-start | bytes 3145732
  180.4 166.6 %copy-start.47 = (f32[128]{0:T(128)S(1)}, f32[128]{0:T(128)}, u32[]{:S(2)}) copy-start(f32[128]{0:T(128)} %copy-done.46) | copy-start | bytes 1540
  180.4 409.3 %reduce-scatter.13.cloned.1.call-start = ((), (), s32[]{:S(2)}) async-start(), calls=%async_computation.12 | async-start | bytes 9437184 | tf_op jit(solution)/shard_map/reduce_scatter | solution.py:355
  346.9 5.5 copy-start.20
  346.9 5.5 copy-start.21
  347.0 5.5 copy-start.58
  347.0 5.5 copy-start.51
  347.0 6.5 copy-start.11
  347.0 6.5 copy-start.15
  347.0 6.5 copy-start.53
  358.4 383.0 %reduce-scatter.15.cloned.1.call-start = ((), (), s32[]{:S(2)}) async-start(), calls=%async_computation.13 | async-start | bytes 9437184 | tf_op jit(solution)/shard_map/reduce_scatter | solution.py:356
  365.6 661.7 %reduce-scatter.21.cloned.1.call-start = ((), (), s32[]{:S(2)}) async-start(), calls=%async_computation.16 | async-start | bytes 18874368 | tf_op jit(solution)/shard_map/reduce_scatter | solution.py:361
  375.1 937.7 %reduce-scatter.23.cloned.1.call-start = ((), (), s32[]{:S(2)}) async-start(), calls=%async_computation.17 | async-start | bytes 18874368 | tf_op jit(solution)/shard_map/reduce_scatter | solution.py:363
  385.0 1138.2 %reduce-scatter.17.cloned.1.call-start = ((), (), s32[]{:S(2)}) async-start(), calls=%async_computation.14 | async-start | bytes 14155776 | tf_op jit(solution)/shard_map/reduce_scatter | solution.py:358
  393.3 1219.7 %all-reduce.9.cloned.1.call-start = ((), (), s32[]{:S(2)}) async-start(), calls=%async_computation.18 | async-start | bytes 8388608 | tf_op jit(solution)/shard_map/psum | solution.py:378
  1030.0 495.6 %copy-start.55 = (bf16[1024]{0:T(1024)(128)(2,1)S(1)}, bf16[1024]{0:T(1024)(128)(2,1)}, u32[]{:S(2)}) copy-start(bf16[1024]{0:T(1024)(128)(2,1)} %param.30) | copy-start | bytes 6148
  1030.0 495.6 %copy-start.61 = (u32[32]{0:T(128)S(1)}, u32[32]{0:T(128)}, u32[]{:S(2)}) copy-start(u32[32]{0:T(128)} %constant.112) | copy-start | bytes 388
  1528.2 5.7 copy-start.43
  1528.2 5.7 copy-start.44
  1612.9 7.0 copy-start.32
  1612.9 7.9 copy-start.26
  1615.2 7.2 copy-start.25
  1617.4 6.5 copy-start.1
  (29 other events, 44.7 us)
Sparse Core Ops, SparseCore 0:
  27.3 53.7 all-gather.3
  83.8 47.4 all-gather.5
  166.5 86.9 reduce-scatter.10
  257.4 88.1 reduce-scatter.8
  349.1 87.8 reduce-scatter.18
  440.9 148.7 reduce-scatter.12
  593.3 147.9 reduce-scatter.14
  745.6 281.6 reduce-scatter.20
  1031.1 281.7 reduce-scatter.22
  1316.7 206.4 reduce-scatter.16
  1527.3 85.5 all-reduce.8
where the time goes:
time: 1640 us; the launch traced here: 1630 us
  waiting for transfers between devices  1380 us (84%)
  matrix products  103 us (6%)
  blocking collectives  63.5 us (4%)
  other arithmetic  41.8 us (3%)
  local copies, waits for them, and re-layouts  25.9 us (2%)
  between operations  16.9 us (1%)
    reduce_scatter x1, waiting for transfers between devices, on_device(): lax.psum_scatter(grad_up, 'seq', scatter_dimension=0, tiled=True)  284 us
    reduce_scatter x1, waiting for transfers between devices, on_device(): lax.psum_scatter(grad_down, 'seq', scatter_dimension=0, tiled=True)  283 us
    reduce_scatter x1, waiting for transfers between devices, on_device(): lax.psum_scatter(grad_qkv, 'seq', scatter_dimension=0, tiled=True)  208 us
    reduce_scatter x1, waiting for transfers between devices, on_device(): lax.psum_scatter(grad_skip_weight, 'seq', scatter_dimension=0, tiled=True)  151 us
    reduce_scatter x1, waiting for transfers between devices, on_device(): lax.psum_scatter(grad_ada, 'seq', scatter_dimension=0, tiled=True)  150 us
    reduce_scatter x1, waiting for transfers between devices, on_device(): lax.psum_scatter(grad_key_all.reshape(total_keys, model_width), 'seq', sc...  90.4 us
    reduce_scatter x1, waiting for transfers between devices, on_device(): lax.psum_scatter(grad_value_all.reshape(total_keys, model_width), 'seq',...  68.4 us
    reduce_scatter x1, waiting for transfers between devices, on_device(): lax.psum_scatter(grad_out_weight, 'seq', scatter_dimension=0, tiled=True)  43.7 us
  transfers between devices with their start and end apart: 11, of which 11 were waited for; matrix products, arithmetic and copies ran while one was open for 6% of the time, Pallas kernels for 0%

commit v1 on v0

--- a/solution.py
+++ b/solution.py
@@ -3,6 +3,8 @@
 import jax
 import jax.numpy as jnp
 from jax import lax
+from jax.experimental import pallas as pl
+from jax.experimental.pallas import tpu as pltpu
 from jax.sharding import PartitionSpec as P
 
 HEADS = 16
@@ -403,6 +405,875 @@
     )
 
 
+RELATIVE = (0, 6, 2, 4, 1, 7, 3, 5)
+STEPS = (1, 2, 6)
+MESH = pl.DeviceIdType.MESH
+MIB = 2**20
+FAR_FIRST = (4, 5, 2, 3, 6, 7, 1)
+ROOT = math.sqrt(2.0 / math.pi)
+
+
+def bit(value, place):
+    return lax.rem(lax.div(value, jnp.int32(1 << place)), jnp.int32(2))
+
+
+def flip(value, mask):
+    out = value
+    for place in range(3):
+        if (mask >> place) & 1:
+            out = out + (1 << place) * (1 - 2 * bit(value, place))
+    return out
+
+
+def exclusive(value, other):
+    return sum(
+        (1 << place) * lax.rem(bit(value, place) + bit(other, place), jnp.int32(2))
+        for place in range(3)
+    )
+
+
+def relative_block(seq_index, number):
+    step_y, step_a, step_b = bit(number, 2), bit(number, 1), bit(number, 0)
+    two = jnp.int32(2)
+    return (
+        lax.rem(bit(seq_index, 0) + step_y, two)
+        + 2 * lax.rem(bit(seq_index, 1) + step_a + step_b, two)
+        + 4 * lax.rem(bit(seq_index, 2) + step_b, two)
+    )
+
+
+def columns(start, size):
+    return pl.ds(pl.multiple_of(start, 128), size)
+
+
+class Links:
+    def __init__(self, send_sems, recv_sems, load_sems):
+        self.send_sems, self.recv_sems, self.load_sems = send_sems, recv_sems, load_sems
+        self.used, self.loads, self.sent = 0, 0, []
+        self.dp_index, self.seq_index = lax.axis_index("dp"), lax.axis_index("seq")
+
+    def peer(self, axis, mask):
+        if axis == "dp":
+            return (flip(self.dp_index, mask), self.seq_index)
+        return (self.dp_index, flip(self.seq_index, mask))
+
+    def barrier(self):
+        semaphore = pltpu.get_barrier_semaphore()
+        for axis, count in (("seq", 8), ("dp", 4)):
+            for mask in range(1, count):
+                pl.semaphore_signal(
+                    semaphore, inc=1, device_id=self.peer(axis, mask), device_id_type=MESH
+                )
+        pl.semaphore_wait(semaphore, 10)
+
+    def send(self, source, target, axis, mask):
+        number = self.used
+        self.used += 1
+        copy = pltpu.make_async_remote_copy(
+            src_ref=source,
+            dst_ref=target,
+            send_sem=self.send_sems.at[number],
+            recv_sem=self.recv_sems.at[number],
+            device_id=self.peer(axis, mask),
+            device_id_type=MESH,
+        )
+        copy.start()
+        self.sent.append(copy)
+        return copy
+
+    def load(self, source, target):
+        copy = pltpu.make_async_copy(source, target, self.load_sems.at[self.loads])
+        self.loads += 1
+        copy.start()
+        return copy
+
+    def settle(self, copy):
+        copy.wait()
+        self.sent = [other for other in self.sent if other is not copy]
+
+    def drain(self):
+        for copy in self.sent:
+            copy.wait_send()
+
+
+def share_start(links, slots):
+    return links.send(slots.at[0], slots.at[2], "dp", 2), links.send(
+        slots.at[0], slots.at[1], "dp", 1
+    )
+
+
+def share_forward(links, slots, copies):
+    copies[0].wait_recv()
+    last = links.send(slots.at[2], slots.at[3], "dp", 1)
+    return copies[1], last
+
+
+def arrived(copies):
+    for copy in copies:
+        copy.wait_recv()
+
+
+def turn_sine_cosine(angles):
+    turns = jnp.floor(angles * (0.5 / math.pi) + 0.5)
+    rest = angles - turns * 6.28125
+    rest = rest - turns * (2.0 * math.pi - 6.28125)
+    return jnp.sin(rest), jnp.cos(rest)
+
+
+def utterance_ends(lengths_ref):
+    ends, total = [], jnp.int32(0)
+    for number in range(lengths_ref.shape[1]):
+        total = total + lengths_ref[0, number]
+        ends.append(total)
+    return ends
+
+
+def segments(ends, index):
+    return sum((index >= end).astype(jnp.int32) for end in ends)
+
+
+def rotary(ends, first_row, rows, width):
+    index = first_row + lax.broadcasted_iota(jnp.int32, (rows, width), 0)
+    start = jnp.zeros_like(index)
+    for end in ends:
+        start = jnp.where(index >= end, end, start)
+    lane = lax.broadcasted_iota(jnp.int32, (rows, width), 1) % HEAD
+    pair = (lane % (HEAD // 2)).astype(jnp.float32)
+    angles = (index - start).astype(jnp.float32) * jnp.exp(
+        pair * (-2.0 * math.log(10000.0) / HEAD)
+    )
+    sine, cosine = turn_sine_cosine(angles)
+    return cosine, jnp.where(lane < HEAD // 2, -sine, sine)
+
+
+def partner(values):
+    half_size = HEAD // 2
+    lane = lax.broadcasted_iota(jnp.int32, values.shape, 1) % HEAD
+    return jnp.where(
+        lane < half_size,
+        pltpu.roll(values, values.shape[1] - half_size, 1),
+        pltpu.roll(values, half_size, 1),
+    )
+
+
+def head_mask(values, head):
+    lane = lax.broadcasted_iota(jnp.int32, values.shape, 1)
+    return jnp.where(lane // HEAD == head, values, jnp.zeros_like(values))
+
+
+def norm_parts(values):
+    centered = values - jnp.mean(values, axis=-1, keepdims=True)
+    variance = jnp.mean(centered * centered, axis=-1, keepdims=True)
+    factor = lax.rsqrt(variance + 1e-06)
+    return centered * factor, factor
+
+
+def norm_back(grad, normal, factor):
+    mean_grad = jnp.mean(grad, axis=-1, keepdims=True)
+    mean_product = jnp.mean(grad * normal, axis=-1, keepdims=True)
+    return factor * (grad - mean_grad - normal * mean_product)
+
+
+def product(left, right):
+    return jnp.dot(left, right, preferred_element_type=jnp.float32)
+
+
+def product_cols(left, right):
+    return lax.dot_general(left, right, contract_cols, preferred_element_type=jnp.float32)
+
+
+def product_rows(left, right):
+    return lax.dot_general(left, right, contract_rows, preferred_element_type=jnp.float32)
+
+
+def first_kernel(
+    lengths, steps, frame_mask, frames, skip, cotangent, b_ada, w_skip, w_ada, w_qkv, w_down,
+    joined_all, cot_all, first_all, embed_all, residual, scale, grad_gated, packed, weights,
+    attn_sum, attn_low,
+    skip_buf, ada_buf, qkv_buf, down_buf, joined_own, first_own, table, packed_send, attn_send,
+    masks, weight_buf, send_sems, recv_sems, load_sems,
+):
+    links = Links(send_sems, recv_sems, load_sems)
+    seq_index, dp_index = links.seq_index, links.dp_index
+    rows, width = frames.shape
+    load_skip = links.load(w_skip, skip_buf)
+    load_ada = links.load(w_ada, ada_buf)
+    load_qkv = links.load(w_qkv, qkv_buf)
+    load_down = links.load(w_down, down_buf)
+
+    block = 2 * width // 8
+    for number in range(8):
+        place = relative_block(seq_index, jnp.int32(number))
+        inside = columns(lax.rem(place, jnp.int32(4)) * block, block)
+        chosen = jnp.where(place < 4, frames[:, inside], skip[:, inside])
+        joined_own[:, number * block : (number + 1) * block] = chosen
+    masks[0] = jnp.broadcast_to(frame_mask[...], masks.shape[1:])
+
+    ends = utterance_ends(lengths)
+    utter = lax.broadcasted_iota(jnp.int32, (16, width), 0)
+    flow = jnp.zeros((16, width), jnp.float32)
+    for number in range(steps.shape[1]):
+        flow = jnp.where(utter == number, steps[0, number].astype(jnp.float32), flow)
+    lane = lax.broadcasted_iota(jnp.int32, (16, width), 1)
+    half = width // 2
+    frequency = jnp.exp(
+        (lane % half).astype(jnp.float32) * (-math.log(10000.0) / half)
+    )
+    sine, cosine = turn_sine_cosine(1000.0 * (flow / TSTEPS) * frequency)
+    embed = jnp.where(lane < half, sine, cosine).astype(jnp.bfloat16)
+    table_embed = embed
+
+    links.barrier()
+    own_copies = [
+        links.load(joined_own, joined_all.at[0]),
+        links.load(cotangent, cot_all.at[0]),
+    ]
+    mask_copies = [links.send(masks.at[0], masks.at[m], "seq", m) for m in range(1, 8)]
+    cot_copies = [
+        links.send(cotangent, cot_all.at[m], "dp", m) for m in (1, 2)
+    ]
+    joined_copies = [links.send(joined_own, joined_all.at[m], "dp", m) for m in (1, 2)]
+
+    load_skip.wait()
+    residual[...] = product(frames[...], skip_buf[:width]) + product(skip[...], skip_buf[width:])
+    load_ada.wait()
+    table[...] = product(table_embed, ada_buf[...]) + b_ada[...].astype(jnp.float32)
+    first_row = seq_index * rows
+    normal, unused = norm_parts(residual[...])
+    row_index = first_row + lax.broadcasted_iota(jnp.int32, (rows, 1), 0)
+    own_segment = segments(ends, row_index)
+    spread_scale = jnp.zeros((rows, width), jnp.float32)
+    spread_shift = jnp.zeros((rows, width), jnp.float32)
+    for number in range(len(ends)):
+        member = own_segment == number
+        spread_scale = jnp.where(member, table[number : number + 1, :width], spread_scale)
+        spread_shift = jnp.where(member, table[number : number + 1, width:], spread_shift)
+    scale[...] = spread_scale
+    first_low = (normal * (1.0 + spread_scale) + spread_shift).astype(jnp.bfloat16)
+    first_own[0] = first_low
+    for number in range(8):
+        place = relative_block(seq_index, jnp.int32(number))
+        first_own[1, :, number * 128 : (number + 1) * 128] = first_own[0, :, columns(place * 128, 128)]
+    own_copies.append(links.load(first_own.at[1], first_all.at[0]))
+    first_copies = [links.send(first_own.at[1], first_all.at[m], "dp", m) for m in (1, 2)]
+
+    cos_own, sin_own = rotary(ends, first_row, rows, 256)
+    load_qkv.wait()
+    packed_copies = {}
+    for far in (2, 1, 3, 0):
+        pair = flip(lax.div(seq_index, jnp.int32(2)), far)
+        parts = []
+        for kind in range(3):
+            part = product(first_low, qkv_buf[:, columns(kind * width + pair * 256, 256)])
+            if kind < 2:
+                part = part * cos_own + partner(part) * sin_own
+            parts.append(part.astype(jnp.bfloat16))
+        for odd in range(2):
+            for kind in range(3):
+                packed_send[pair * 2 + odd, :, kind * 128 : (kind + 1) * 128] = parts[kind][
+                    :, odd * 128 : (odd + 1) * 128
+                ]
+        for mask in (2 * far, 2 * far + 1):
+            if mask:
+                packed_copies[mask] = links.send(
+                    packed_send.at[flip(seq_index, mask)], packed.at[seq_index], "seq", mask
+                )
+    packed[seq_index] = packed_send[seq_index]
+
+    forwards = []
+    for slots, copies in ((cot_all, cot_copies), (joined_all, joined_copies)):
+        copies[1].wait_recv()
+        forwards.append(links.send(slots.at[2], slots.at[3], "dp", 1))
+    load_down.wait()
+
+    def gated_step(step, carried):
+        part = columns(step * 512, 512)
+        grad_gated[:, part] = product_cols(cotangent[...], down_buf[part, :])
+        return carried
+
+    lax.fori_loop(0, down_buf.shape[0] // 512, gated_step, 0)
+    embed_own = first_own.at[2, :16]
+    embed_own[...] = embed
+    own_copies.append(links.load(embed_own, embed_all.at[0]))
+    embed_copies = [links.send(embed_own, embed_all.at[m], "dp", m) for m in range(1, 4)]
+    first_copies[1].wait_recv()
+    forwards.append(links.send(first_all.at[2], first_all.at[3], "dp", 1))
+
+    arrived(mask_copies)
+    arrived(packed_copies.values())
+    key_index = lax.broadcasted_iota(jnp.int32, (1, 8 * rows), 1)
+    key_segment = segments(ends, key_index)
+    key_valid = jnp.concatenate(
+        [
+            masks[exclusive(seq_index, jnp.int32(number))][:1]
+            for number in range(8)
+        ],
+        axis=1,
+    )
+
+    def attend(place):
+        query = packed[place, :, :128]
+        row_index = place * rows + lax.broadcasted_iota(jnp.int32, (rows, 1), 0)
+        allowed = (segments(ends, row_index) == key_segment) & (
+            (key_valid > 0) | (row_index == key_index)
+        )
+        keys = packed[:, :, 128:256].reshape(8 * rows, 128)
+        values = packed[:, :, 256:].reshape(8 * rows, 128)
+        total = jnp.zeros((rows, 128), jnp.float32)
+        here = pl.ds(pl.multiple_of(place * rows, rows), rows)
+        for head in range(2):
+            scores = product_cols(head_mask(query, head), keys) * (1.0 / math.sqrt(HEAD))
+            scores = jnp.where(allowed, scores, masked_score)
+            raised = jnp.exp(scores - jnp.max(scores, axis=1, keepdims=True))
+            low = (raised / jnp.sum(raised, axis=1, keepdims=True)).astype(jnp.bfloat16)
+            weight_buf[here, head * 1024 : (head + 1) * 1024] = low
+            total = total + product(low, head_mask(values, head))
+        attn_sum[here, :] = total
+        attn_send[place] = total.astype(jnp.bfloat16)
+
+    base = links.used
+
+    def attn_copy(mask):
+        target = exclusive(seq_index, mask)
+        return pltpu.make_async_remote_copy(
+            src_ref=attn_send.at[target],
+            dst_ref=attn_low.at[seq_index],
+            send_sem=send_sems.at[base + mask],
+            recv_sem=recv_sems.at[base + mask],
+            device_id=(dp_index, target),
+            device_id_type=MESH,
+        )
+
+    def attend_step(step, carried):
+        mask = 7 - step
+        attend(exclusive(seq_index, mask))
+        attn_copy(mask).start()
+        return carried
+
+    lax.fori_loop(0, 7, attend_step, 0)
+    attend(seq_index)
+    save = links.load(weight_buf, weights)
+    own = pltpu.make_async_copy(
+        attn_send.at[seq_index], attn_low.at[seq_index], load_sems.at[links.loads]
+    )
+    own.start()
+    arrived(cot_copies[:1] + joined_copies[:1] + first_copies[:1] + embed_copies + forwards)
+    links.drain()
+    for mask in range(1, 8):
+        attn_copy(jnp.int32(mask)).wait()
+    save.wait()
+    own.wait()
+    for copy in own_copies:
+        copy.wait()
+
+
+def second_kernel(
+    lengths, b_up, b_down, gain, joined_in, cot_in, first_in, residual_in, scale_in, gated_in,
+    packed_in, weights_in, attn_sum_in, attn_low_in, w_out, w_up, w_down, w_qkv, w_skip,
+    result, grad_frames, grad_skip, sum_skip, sum_qkv, sum_out, sum_up, sum_down, small_all,
+    out_buf, up_buf, down_buf, weight_buf, attn_sum, packed, attn_low, joined_all, cot_all,
+    first_all, attn_all, second_all, gated_all, upper_all, branch_all, packed_all, in_all,
+    residual, scale, grad_gated, second_low, gated, gated_parts, upper_parts, residual_mid, normal_mid, grad_mid,
+    branch, grad_send, grad_heads, back_send, back_recv, grad_packed, grad_in, key_total, value_total,
+    small, small_recv,
+    down_send, down_recv, down_a, down_b, up_send, up_recv, up_a, up_b, out_send, out_recv, out_a, out_b,
+    qkv_send, qkv_recv, qkv_a, qkv_b, skip_send, skip_recv, skip_a, skip_b,
+    send_sems, recv_sems, load_sems,
+):
+    links = Links(send_sems, recv_sems, load_sems)
+    seq_index, dp_index = links.seq_index, links.dp_index
+    rows, width = residual.shape
+    hidden = grad_gated.shape[1]
+    float32, bfloat16 = jnp.float32, jnp.bfloat16
+    load_attn = links.load(attn_low_in, attn_low)
+    load_out = links.load(w_out, out_buf)
+    load_residual = links.load(residual_in, residual)
+    load_up = links.load(w_up, up_buf)
+    load_gated = links.load(gated_in, grad_gated)
+    load_cot = links.load(cot_in, cot_all)
+    load_down = links.load(w_down, down_buf)
+    load_packed = links.load(packed_in, packed)
+    load_sum = links.load(attn_sum_in, attn_sum)
+    load_weights = links.load(weights_in, weight_buf)
+    load_scale = links.load(scale_in, scale)
+    load_first = links.load(first_in, first_all)
+    load_joined = links.load(joined_in, joined_all)
+    links.barrier()
+
+    def relative(source, target):
+        for number in range(8):
+            place = relative_block(seq_index, jnp.int32(number))
+            target[0, :, number * 128 : (number + 1) * 128] = source[:, columns(place * 128, 128)]
+
+    load_attn.wait()
+    for number in range(8):
+        place = relative_block(seq_index, jnp.int32(number))
+        attn_all[0, :, number * 128 : (number + 1) * 128] = attn_low[place]
+    attn_copies = share_start(links, attn_all)
+    load_out.wait()
+    load_residual.wait()
+    joined_attn = jnp.concatenate([attn_low[number] for number in range(8)], axis=1)
+    residual_mid[...] = residual[...] + product(joined_attn, out_buf[...])
+    normal, factor_mid = norm_parts(residual_mid[...])
+    normal_mid[...] = normal
+    gain_float = gain[...].astype(float32)
+    second_low[...] = (normal * gain_float).astype(bfloat16)
+    relative(second_low, second_all)
+    second_copies = share_start(links, second_all)
+    small[8:] = jnp.zeros((8, small.shape[1]), float32)
+    load_up.wait()
+    load_gated.wait()
+
+    def up_step(step, carried):
+        number = lax.rem(step + 4, jnp.int32(8))
+        place = relative_block(seq_index, number)
+        part = columns(place * 512, 512)
+        upper = product(second_low[...], up_buf[:, part]) + b_up[:, part].astype(float32)
+        square = upper * upper
+        bent = jnp.tanh(ROOT * (upper + 0.044715 * upper * square))
+        low = (0.5 * upper * (1.0 + bent)).astype(bfloat16)
+        slope = 0.5 * (1.0 + bent) + 0.5 * upper * (1.0 - bent * bent) * ROOT * (
+            1.0 + 3.0 * 0.044715 * square
+        )
+        grad_upper = (grad_gated[:, part] * slope).astype(bfloat16)
+        gated[:, part] = low
+        for quarter in range(4):
+            gated_parts[quarter, :, columns(number * 128, 128)] = low[
+                :, quarter * 128 : (quarter + 1) * 128
+            ]
+        upper_parts[lax.div(place, jnp.int32(2)), :, columns(bit(place, 0) * 512, 512)] = grad_upper
+        small[
+            pl.ds(8 + lax.div(place, jnp.int32(4)), 1),
+            columns(lax.rem(place, jnp.int32(4)) * 512, 512),
+        ] = jnp.sum(grad_upper.astype(float32), axis=0, keepdims=True)
+        return carried
+
+    lax.fori_loop(0, 8, up_step, 0)
+    gated_copies = [
+        links.send(gated_parts.at[flip(dp_index, m)], gated_all.at[m], "dp", m) for m in (3, 2, 1)
+    ]
+    upper_copies = [
+        links.send(upper_parts.at[flip(dp_index, m)], upper_all.at[m], "dp", m) for m in (3, 2, 1)
+    ]
+    gated_all[0] = gated_parts[dp_index]
+    upper_all[0] = upper_parts[dp_index]
+    attn_copies = share_forward(links, attn_all, attn_copies)
+    second_copies = share_forward(links, second_all, second_copies)
+
+    key_total[...] = jnp.zeros_like(key_total)
+    value_total[...] = jnp.zeros_like(value_total)
+
+    def second_step(step, total):
+        return total + product_cols(
+            upper_parts[lax.div(step, jnp.int32(2)), :, columns(bit(step, 0) * 512, 512)],
+            up_buf[:, columns(step * 512, 512)],
+        )
+
+    grad_second = lax.fori_loop(0, 8, second_step, jnp.zeros((rows, width), float32))
+    load_qkv = links.load(w_qkv, up_buf.at[:, : 3 * width])
+    load_cot.wait()
+    grad_out = cot_all[0].astype(float32)
+    normal = normal_mid[...]
+    small[10:11, :width] = jnp.sum(grad_second * normal, axis=0, keepdims=True)
+    small[10:11, width:] = jnp.sum(grad_out, axis=0, keepdims=True)
+    grad_mid[...] = grad_out + norm_back(grad_second * gain_float, normal, factor_mid)
+    branch[...] = grad_mid[...].astype(bfloat16)
+    branch_copies = [
+        links.send(branch.at[:, columns(flip(dp_index, m) * 256, 256)], branch_all.at[m], "dp", m)
+        for m in (3, 2, 1)
+    ]
+    branch_all[0] = branch[:, columns(dp_index * 256, 256)]
+    grad_attn = product_cols(branch[...], out_buf[...]).astype(bfloat16)
+    for number in range(8):
+        grad_send[number] = grad_attn[:, number * 128 : (number + 1) * 128]
+    head_copies = [
+        links.send(grad_send.at[flip(seq_index, m)], grad_heads.at[seq_index], "seq", m)
+        for m in FAR_FIRST
+    ]
+    grad_heads[seq_index] = grad_send[seq_index]
+
+    def piece(left, right, start, size):
+        return product_rows(
+            left[:, :, columns(start, size)].reshape(4 * rows, size),
+            right[...].reshape(4 * rows, right.shape[2]),
+        )
+
+    class Sum:
+        def __init__(self, left, right, send, recv, recv_a, recv_b):
+            self.left, self.right, self.out, self.into = left, right, send, recv
+            self.into_a, self.into_b = recv_a, recv_b
+            self.half = send.shape[0]
+            self.size = self.half // 4
+
+        def begin(self):
+            def step(number, carried):
+                start = pl.multiple_of(number * 256, 256)
+                self.out[pl.ds(start, 256), :] = piece(
+                    self.left, self.right, self.half + start, 256
+                ).astype(bfloat16)
+                return carried
+
+            lax.fori_loop(0, self.half // 256, step, 0)
+            self.copy = links.send(self.out, self.into, "seq", STEPS[0])
+
+        def part(self, low, high):
+            def step(number, carried):
+                start = pl.multiple_of(number * 256, 256)
+                here = pl.ds(start, 256)
+                self.out[here, :] = (
+                    piece(self.left, self.right, start, 256) + self.into[here, :].astype(float32)
+                ).astype(bfloat16)
+                return carried
+
+            lax.fori_loop(low // 256, high // 256, step, 0)
+
+        def second(self):
+            links.settle(self.copy)
+            self.part(2 * self.size, 4 * self.size)
+            self.copy = links.send(
+                self.out.at[2 * self.size :], self.into_a, "seq", STEPS[1]
+            )
+            self.part(0, 2 * self.size)
+
+        def third(self):
+            self.copy.wait_recv()
+            both = pl.ds(0, 2 * self.size)
+            self.into[both, :] = (
+                self.out[both, :].astype(float32) + self.into_a[...].astype(float32)
+            ).astype(bfloat16)
+            self.copy = links.send(
+                self.into.at[self.size : 2 * self.size], self.into_b, "seq", STEPS[2]
+            )
+
+        def last(self, target, spread):
+            self.copy.wait_recv()
+            own = pl.ds(0, self.size)
+            self.out[own, :] = (
+                self.into[own, :].astype(float32) + self.into_b[...].astype(float32)
+            ).astype(bfloat16)
+
+            def place(index):
+                if spread == 0:
+                    return target.at[pl.ds(index * self.size, self.size), :]
+                size = self.out.shape[1]
+                return target.at[:, columns(index * size, size)]
+
+            self.target = place
+            ready = self.out.at[: self.size]
+            self.across = links.send(ready, place(dp_index), "dp", 2)
+            self.core = links.send(ready, place(dp_index), "dp", 1)
+            self.own = links.load(ready, place(dp_index))
+
+        def spread(self):
+            self.across.wait_recv()
+            other = self.target(flip(dp_index, 2))
+            self.far = links.send(other, other, "dp", 1)
+
+        def finish(self):
+            self.own.wait()
+            arrived([self.core, self.far])
+
+    down = Sum(gated_all, cot_all, down_send, down_recv, down_a, down_b)
+    up = Sum(second_all, upper_all, up_send, up_recv, up_a, up_b)
+    out = Sum(attn_all, branch_all, out_send, out_recv, out_a, out_b)
+    qkv = Sum(first_all, packed_all, qkv_send, qkv_recv, qkv_a, qkv_b)
+    skip = Sum(joined_all, in_all, skip_send, skip_recv, skip_a, skip_b)
+
+    arrived(gated_copies)
+    down.begin()
+    arrived(upper_copies)
+    arrived(second_copies)
+    up.begin()
+    load_down.wait()
+
+    def down_step(step, total):
+        part = columns(step * 512, 512)
+        return total + product(gated[:, part], down_buf[part, :])
+
+    lower = lax.fori_loop(
+        0, 8, down_step, residual_mid[...] + b_down[...].astype(float32)
+    )
+    result[...] = lower.astype(bfloat16)
+    load_skip = links.load(w_skip, down_buf.at[: 2 * width])
+    arrived(branch_copies)
+    arrived(attn_copies)
+    out.begin()
+
+    ends = utterance_ends(lengths)
+    load_packed.wait()
+    load_sum.wait()
+    load_weights.wait()
+    arrived(head_copies)
+    shrink = 1.0 / math.sqrt(HEAD)
+
+    def back_step(place, carried):
+        here = pl.ds(pl.multiple_of(place * rows, rows), rows)
+        grad = grad_heads[place]
+        query = packed[place, :, :128]
+        keys = packed[:, :, 128:256].reshape(8 * rows, 128)
+        values = packed[:, :, 256:].reshape(8 * rows, 128)
+        both = grad.astype(float32) * attn_sum[here, :]
+        total = jnp.zeros((rows, 128), float32)
+        for head in range(2):
+            low = weight_buf[here, head * 1024 : (head + 1) * 1024]
+            grad_head = head_mask(grad, head)
+            delta = jnp.sum(head_mask(both, head), axis=1, keepdims=True)
+            grad_scores = (
+                low.astype(float32) * (product_cols(grad_head, values) - delta)
+            ).astype(bfloat16)
+            total = total + product(grad_scores, head_mask(keys, head))
+            key_total[...] += product_rows(grad_scores, head_mask(query, head))
+            value_total[...] += product_rows(low, grad_head)
+        total = total * shrink
+        cosine, sine = rotary(ends, place * rows, rows, 128)
+        back_send[place, :, :128] = (total * cosine - partner(total) * sine).astype(bfloat16)
+        return carried
+
+    lax.fori_loop(0, 8, back_step, 0)
+
+    def key_step(place, carried):
+        here = pl.ds(pl.multiple_of(place * rows, rows), rows)
+        total = key_total[here, :] * shrink
+        cosine, sine = rotary(ends, place * rows, rows, 128)
+        back_send[place, :, 128:256] = (total * cosine - partner(total) * sine).astype(bfloat16)
+        back_send[place, :, 256:] = value_total[here, :].astype(bfloat16)
+        return carried
+
+    lax.fori_loop(0, 8, key_step, 0)
+    back_copies = [
+        links.send(back_send.at[flip(seq_index, m)], back_recv.at[seq_index], "seq", m)
+        for m in FAR_FIRST
+    ]
+    back_recv[seq_index] = back_send[seq_index]
+    down.second()
+    up.second()
+    out.second()
+
+    arrived(back_copies)
+    for number in range(8):
+        for kind in range(3):
+            grad_packed[:, kind * width + number * 128 : kind * width + (number + 1) * 128] = (
+                back_recv[number, :, kind * 128 : (kind + 1) * 128]
+            )
+    packed_copies = [
+        links.send(
+            grad_packed.at[:, columns(flip(dp_index, m) * 768, 768)], packed_all.at[m], "dp", m
+        )
+        for m in (3, 2, 1)
+    ]
+    packed_all[0] = grad_packed[:, columns(dp_index * 768, 768)]
+    load_qkv.wait()
+
+    def first_step(step, total):
+        part = columns(step * 512, 512)
+        return total + product_cols(grad_packed[:, part], up_buf[:, part])
+
+    grad_first = lax.fori_loop(0, 6, first_step, jnp.zeros((rows, width), float32))
+    normal, factor = norm_parts(residual[...])
+    load_scale.wait()
+    grad_in[...] = (
+        grad_mid[...] + norm_back(grad_first * (1.0 + scale[...]), normal, factor)
+    ).astype(bfloat16)
+    in_copies = [
+        links.send(grad_in.at[:, columns(flip(dp_index, m) * 256, 256)], in_all.at[m], "dp", m)
+        for m in (3, 2, 1)
+    ]
+    in_all[0] = grad_in[:, columns(dp_index * 256, 256)]
+    row_index = seq_index * rows + lax.broadcasted_iota(jnp.int32, (rows, 1), 0)
+    own_segment = segments(ends, row_index)
+    scaled = grad_first * normal
+    for number in range(len(ends)):
+        member = own_segment == number
+        small[number : number + 1, :width] = jnp.sum(
+            jnp.where(member, scaled, 0.0), axis=0, keepdims=True
+        )
+        small[number : number + 1, width:] = jnp.sum(
+            jnp.where(member, grad_first, 0.0), axis=0, keepdims=True
+        )
+    small_copy = links.send(small, small_recv.at[0], "seq", STEPS[0])
+    load_first.wait()
+    arrived(packed_copies)
+    qkv.begin()
+    load_joined.wait()
+    arrived(in_copies)
+    skip.begin()
+    down.third()
+    up.third()
+    out.third()
+    load_skip.wait()
+    for target, start in ((grad_frames, 0), (grad_skip, width)):
+        target[...] = product_cols(grad_in[...], down_buf[start : start + width, :])
+    links.settle(small_copy)
+    small[...] = small[...] + small_recv[0]
+    small_copy = links.send(small, small_recv.at[1], "seq", STEPS[1])
+    down.last(sum_down, 0)
+    up.last(sum_up, 1)
+    out.last(sum_out, 1)
+    qkv.second()
+    skip.second()
+    links.settle(small_copy)
+    small[...] = small[...] + small_recv[1]
+    small_copy = links.send(small, small_recv.at[2], "seq", STEPS[2])
+    down.spread()
+    up.spread()
+    out.spread()
+    qkv.third()
+    skip.third()
+    links.settle(small_copy)
+    small[...] = small[...] + small_recv[2]
+    small_across = links.send(small, small_all.at[dp_index], "dp", 2)
+    small_core = links.send(small, small_all.at[dp_index], "dp", 1)
+    small_far = links.send(small, small_all.at[dp_index], "dp", 3)
+    small_own = links.load(small, small_all.at[dp_index])
+    qkv.last(sum_qkv, 1)
+    skip.last(sum_skip, 1)
+    qkv.spread()
+    skip.spread()
+    small_own.wait()
+    arrived([small_across, small_core, small_far])
+    for each in (down, up, out, qkv, skip):
+        each.finish()
+    links.drain()
+
+
+def two_kernels(
+    frames, skip, lengths, frame_mask, time_step, w_skip, w_ada, b_ada, w_qkv, w_out, norm_gain,
+    w_up, b_up, w_down, b_down, cotangent,
+):
+    rows, width = frames.shape[1:]
+    hidden = b_up.shape[0]
+    seq_index = lax.axis_index("seq")
+    float32, bfloat16 = jnp.float32, jnp.bfloat16
+    shape = jax.ShapeDtypeStruct
+    vmem = pl.BlockSpec(memory_space=pltpu.VMEM)
+    smem = pl.BlockSpec(memory_space=pltpu.SMEM)
+    anywhere = pl.BlockSpec(memory_space=pl.ANY)
+    dma = pltpu.SemaphoreType.DMA
+
+    first_outs = (
+        (shape((4, rows, 2 * width), bfloat16), anywhere),
+        (shape((4, rows, width), bfloat16), anywhere),
+        (shape((4, rows, width), bfloat16), anywhere),
+        (shape((4, 16, width), bfloat16), anywhere),
+        (shape((rows, width), float32), vmem),
+        (shape((rows, width), float32), vmem),
+        (shape((rows, hidden), float32), vmem),
+        (shape((8, rows, 384), bfloat16), vmem),
+        (shape((8 * rows, 2048), bfloat16), anywhere),
+        (shape((8 * rows, 128), float32), vmem),
+        (shape((8, rows, 128), bfloat16), anywhere),
+    )
+    (
+        joined_all, cot_all, first_all, embed_all, residual, scale, grad_gated, packed, weights,
+        attn_sum, attn_low,
+    ) = pl.pallas_call(
+        first_kernel,
+        out_shape=tuple(item[0] for item in first_outs),
+        in_specs=[smem, smem, vmem, vmem, vmem, vmem, vmem, anywhere, anywhere, anywhere, anywhere],
+        out_specs=tuple(item[1] for item in first_outs),
+        scratch_shapes=[
+            pltpu.VMEM(w_skip.shape, bfloat16),
+            pltpu.VMEM(w_ada.shape, bfloat16),
+            pltpu.VMEM(w_qkv.shape, bfloat16),
+            pltpu.VMEM(w_down.shape, bfloat16),
+            pltpu.VMEM((rows, 2 * width), bfloat16),
+            pltpu.VMEM((3, rows, width), bfloat16),
+            pltpu.VMEM((16, 2 * width), float32),
+            pltpu.VMEM((8, rows, 384), bfloat16),
+            pltpu.VMEM((8, rows, 128), bfloat16),
+            pltpu.VMEM((8, 8, rows), jnp.int32),
+            pltpu.VMEM((8 * rows, 2048), bfloat16),
+            dma((48,)),
+            dma((48,)),
+            dma((12,)),
+        ],
+        compiler_params=pltpu.CompilerParams(
+            collective_id=0, has_side_effects=True, vmem_limit_bytes=58 * MIB
+        ),
+        name="first",
+    )(
+        lengths, time_step, frame_mask, frames[0], skip[0], cotangent[0], b_ada[None], w_skip,
+        w_ada, w_qkv, w_down,
+    )
+
+    sums = ((1024, 1024), (1024, 1024), (1024, 256), (1024, 768), (2048, 256))
+    sum_scratch = []
+    for tall, wide in sums:
+        sum_scratch += [pltpu.VMEM((tall // part, wide), bfloat16) for part in (2, 2, 4, 8)]
+    second_outs = (
+        (shape((rows, width), bfloat16), vmem),
+        (shape((rows, width), float32), vmem),
+        (shape((rows, width), float32), vmem),
+        (shape((2 * width // 8, width), bfloat16), anywhere),
+        (shape((width // 8, 3 * width), bfloat16), anywhere),
+        (shape((width // 8, width), bfloat16), anywhere),
+        (shape((width // 8, hidden), bfloat16), anywhere),
+        (shape((hidden // 8, width), bfloat16), anywhere),
+        (shape((4, 16, 2 * width), float32), anywhere),
+    )
+    low = lambda *size: pltpu.VMEM(size, bfloat16)
+    full = lambda *size: pltpu.VMEM(size, float32)
+    (
+        result, grad_frames, grad_skip, sum_skip, sum_qkv, sum_out, sum_up, sum_down, small_all,
+    ) = pl.pallas_call(
+        second_kernel,
+        out_shape=tuple(item[0] for item in second_outs),
+        in_specs=[smem, vmem, vmem, vmem] + [anywhere] * 15,
+        out_specs=tuple(item[1] for item in second_outs),
+        scratch_shapes=[
+            low(*w_out.shape), low(*w_up.shape), low(*w_down.shape), low(8 * rows, 2048),
+            full(8 * rows, 128), low(8, rows, 384), low(8, rows, 128),
+            low(4, rows, 2 * width), low(4, rows, width), low(4, rows, width),
+            low(4, rows, width), low(4, rows, width), low(4, rows, width), low(4, rows, width),
+            low(4, rows, 256), low(4, rows, 768), low(4, rows, 256),
+            full(rows, width), full(rows, width), full(rows, hidden), low(rows, width),
+            low(rows, hidden), low(4, rows, width), low(4, rows, width),
+            full(rows, width), full(rows, width), full(rows, width),
+            low(rows, width), low(8, rows, 128), low(8, rows, 128), low(8, rows, 384), low(8, rows, 384),
+            low(rows, 3 * width), low(rows, width), full(8 * rows, 128), full(8 * rows, 128),
+            full(16, 2 * width), full(3, 16, 2 * width),
+            *sum_scratch,
+            dma((90,)), dma((90,)), dma((24,)),
+        ],
+        compiler_params=pltpu.CompilerParams(
+            collective_id=1, has_side_effects=True, vmem_limit_bytes=60 * MIB
+        ),
+        name="second",
+    )(
+        lengths, b_up[None], b_down[None], norm_gain[None], joined_all, cot_all, first_all,
+        residual, scale, grad_gated, packed, weights, attn_sum, attn_low, w_out, w_up, w_down,
+        w_qkv, w_skip,
+    )
+
+    dp_index = lax.axis_index("dp")
+    embed_ordered = jnp.stack(
+        [lax.dynamic_index_in_dim(embed_all, dp_index ^ number, 0, False) for number in range(4)]
+    )
+    count_utter = lengths.shape[1]
+    ada_all = small_all[:, :count_utter].reshape(-1, 2 * width)
+    vectors = jnp.sum(small_all[:, count_utter:], axis=0)
+    own_embed = lax.dynamic_slice_in_dim(embed_ordered, seq_index * 128, 128, axis=2)
+    own_embed = own_embed[:, :count_utter].reshape(-1, 128).astype(float32)
+    total_ada = lax.dot_general(own_embed, ada_all, contract_rows, precision=precise)
+    bias = lambda values, size: lax.dynamic_slice_in_dim(values, seq_index * size, size)
+    wide = lambda values: values.astype(float32)
+    return (
+        result[None],
+        grad_frames[None],
+        grad_skip[None],
+        wide(sum_skip),
+        total_ada,
+        bias(jnp.sum(ada_all, axis=0), 256),
+        wide(sum_qkv),
+        wide(sum_out),
+        bias(vectors[2, :width], 128),
+        wide(sum_up),
+        bias(vectors[:2].reshape(-1), 512),
+        wide(sum_down),
+        bias(vectors[2, width:], 128),
+    )
+
+
 def solution(mesh):
     placed = (
         P("dp", "seq", None),
@@ -422,8 +1293,9 @@
         P(),
         P("dp", "seq", None),
     )
+    split_heads = mesh.shape["dp"] == 4 and mesh.shape["seq"] == len(RELATIVE)
     return jax.shard_map(
-        on_device,
+        two_kernels if split_heads else on_device,
         mesh=mesh,
         in_specs=placed,
         out_specs=(

time: 1640 us -> 232 us (0.14)
  waiting for transfers between devices: 1380 us -> 0 us
  Pallas kernels: 0 us -> 210 us
  matrix products: 103 us -> 2.55 us
  blocking collectives: 63.5 us -> 0 us
  other arithmetic: 41.8 us -> 8.76 us
  local copies, waits for them, and re-layouts: 25.9 us -> 7.27 us
    reduce_scatter x8 -> x0, waiting for transfers between devices: 1280 us -> none  [the longest x1 284 us: on_device(): lax.psum_scatter(grad_up, 'seq', scatter_dimension=0, tiled=True)]
    pallas_call x0 -> x2, Pallas kernels: none -> 210 us  [the longest x1 165 us: two_kernels(): pl.pallas_call(second_kernel, out_shape=tuple((item[0] for item in second...]
    dot_general x25 -> x1, matrix products: 103 us -> 2.55 us  [two_kernels(): lax.dot_general(own_embed, ada_all, contract_rows, precision=precise)]
    all_gather x2 -> x0, waiting for transfers between devices: 70.6 us -> none  [the longest x1 42.9 us: on_device(): lax.all_gather(values_low, 'seq', axis=0, tiled=True)]
    unnamed x1 -> x0, blocking collectives: 35.2 us -> none
    psum x1 -> x0, waiting for transfers between devices: 30.8 us -> none  [on_device(): lax.psum(share_skip.astype(jnp.bfloat16), 'dp').astype(jnp.float32)]
    all_gather x1 -> x0, blocking collectives: 22.7 us -> none  [on_device(): lax.all_gather(valid_low, 'seq', axis=0, tiled=True)]
    convert_element_type x24 -> x5, other arithmetic: 28.6 us -> 7.61 us  [two_kernels(): wide = lambda values: values.astype(float32)]
  transfers between devices with their start and end apart: 11 -> 0, of which waited for: 11 -> 0; matrix products, arithmetic and copies ran while one was open for 6% -> 0% of each run, Pallas kernels for 0% -> 0%
where the time goes in v1:
time: 232 us; the launch traced here: 230 us
  Pallas kernels  210 us (91%)
  other arithmetic  8.76 us (4%)
  local copies, waits for them, and re-layouts  7.27 us (3%)
  matrix products  2.55 us (1%)
    pallas_call x1, Pallas kernels, two_kernels(): pl.pallas_call(second_kernel, out_shape=tuple((item[0] for item in second...  165 us
    pallas_call x1, Pallas kernels, two_kernels(): pl.pallas_call(first_kernel, out_shape=tuple((item[0] for item in first_o...  45.9 us
    convert_element_type x5, other arithmetic, two_kernels(): wide = lambda values: values.astype(float32)  7.61 us

profile of v1, /device:TPU:0, one launch (start us, length us, event | category | flops | bytes accessed | tf_op | source)
XLA Modules:
  0.0 229.8 jit_solution(8415281883791038080)
XLA Ops:
  0.6 1.3 broadcast_in_dim.24.b_ada
  1.9 0.0 copy-start.8
  1.9 0.0 copy-start.9
  1.9 0.0 copy-start.10
  1.9 45.9 %first.1 = (bf16[4,128,2048]{2,1,0:T(8,128)(2,1)}, bf16[4,128,1024]{2,1,0:T(8,128)(2,1)}, bf16[4,128,1024]{2,1,0:T(8,128)(2,1)}, bf16[4,16,1024]{2,1,0:T(8,128)(...) custom-call(s32[1,8]{1,0:T(1,128)} %lengths.3, ...), custom_call_target="tpu_custom_call" | custom-call | tf_op jit(solution)/shard_map/first/pallas_call | solution.py:1169
  47.9 0.0 copy-done.8
  47.9 0.6 broadcast_in_dim.21.b_up
  48.5 0.0 copy-done.9
  48.5 0.6 broadcast_in_dim.22.b_down
  49.1 0.0 copy-done.10
  49.1 0.6 broadcast_in_dim.23.gain
  49.7 0.0 copy-start.7
  49.7 164.5 %second.1 = (bf16[128,1024]{1,0:T(8,128)(2,1)}, f32[128,1024]{1,0:T(8,128)}, f32[128,1024]{1,0:T(8,128)}, bf16[256,1024]{1,0:T(8,128)(2,1)}, bf16[128,3072]{1,0:...) custom-call(s32[1,8]{1,0:T(1,128)} %lengths.3, ...), custom_call_target="tpu_custom_call" | custom-call | tf_op jit(solution)/shard_map/second/pallas_call | solution.py:1218
  214.2 0.0 copy-start
  214.2 1.2 slice_reduce_fusion
  215.4 0.0 copy-start.1
  215.4 0.5 fusion.8
  216.0 0.0 copy-done.7
  216.0 2.5 %convolution_bitcast_fusion = f32[128,2048]{1,0:T(8,128)} fusion(f32[4,16,2048]{2,1,0:T(8,128)} %get-tuple-element.48, s32[]{:T(128)S(6)} %select_n.28, bf16[1,16,1024]{2,1,0:T(8,128)(2,1)S(1)} %get-tuple-element.56, bf16[1,16,1024]{2,1,0:T(8,128)(2,1)S(1)} %get-tuple-element.57, bf16[1,16,1024]{2,1,0:T(8,128)(2,1)S(1)} %get-tuple-element.58, ...), kind=kOutput, calls=%fused_computation | convolution fusion | flops 100696064 | bytes 1441796 | tf_op jit(solution)/shard_map/dot_general | solution.py:1257
  218.5 0.7 dynamic_slice.40
  219.2 0.6 dynamic_slice.37
  219.8 0.0 copy-start.2
  219.8 2.8 %convert_element_type.19 = f32[128,4096]{1,0:T(8,128)} convert(bf16[128,4096]{1,0:T(8,128)(2,1)} %get-tuple-element.51) | non-fusion elementwise | flops 524288 | bytes 3145728 | tf_op jit(solution)/shard_map/convert_element_type | solution.py:1259
  222.6 0.0 copy-start.5
  222.6 0.0 copy-start.6
  222.7 0.0 copy-done
  222.7 0.0 copy-start.4
  222.7 0.0 copy-start.3
  222.7 1.6 convert_element_type.20
  224.2 0.0 copy-done.1
  224.2 1.3 convert_element_type.17
  225.5 0.0 copy-done.2
  225.5 1.1 convert_element_type.16
  226.6 0.0 copy-done.5
  226.6 0.8 convert_element_type.18
  227.5 0.0 copy-done.6
  227.5 0.7 copy.33
  228.2 0.0 copy-done.4
  228.2 0.8 copy.34
  229.0 0.0 copy-done.3
  229.0 0.8 copy.35
  (4 shorter events, 0.0 us)
Async XLA Ops:
  1.9 45.9 %copy-start.8 = (bf16[4096]{0:T(1024)(128)(2,1)S(1)}, bf16[4096]{0:T(1024)(128)(2,1)}, u32[]{:S(2)}) copy-start(bf16[4096]{0:T(1024)(128)(2,1)} %param.28) | copy-start | bytes 24580
  1.9 46.5 %copy-start.9 = (bf16[1024]{0:T(1024)(128)(2,1)S(1)}, bf16[1024]{0:T(1024)(128)(2,1)}, u32[]{:S(2)}) copy-start(bf16[1024]{0:T(1024)(128)(2,1)} %param.30) | copy-start | bytes 6148
  1.9 47.1 %copy-start.10 = (bf16[1024]{0:T(1024)(128)(2,1)S(1)}, bf16[1024]{0:T(1024)(128)(2,1)}, u32[]{:S(2)}) copy-start(bf16[1024]{0:T(1024)(128)(2,1)} %param.26) | copy-start | bytes 6148
  49.7 166.3 %copy-start.7 = (bf16[4,16,1024]{2,1,0:T(8,128)(2,1)S(1)}, bf16[4,16,1024]{2,1,0:T(8,128)(2,1)}, u32[]{:S(2)}) copy-start(bf16[4,16,1024]{2,1,0:T(8,128)(2,1)} %get-tuple-element.47) | copy-start | bytes 393220
  214.2 8.4 %copy-start = (bf16[512,1024]{1,0:T(8,128)(2,1)S(1)}, bf16[512,1024]{1,0:T(8,128)(2,1)}, u32[]{:S(2)}) copy-start(bf16[512,1024]{1,0:T(8,128)(2,1)} %get-tuple-element.52) | copy-start | bytes 3145732
  215.4 8.8 %copy-start.1 = (bf16[128,3072]{1,0:T(8,128)(2,1)S(1)}, bf16[128,3072]{1,0:T(8,128)(2,1)}, u32[]{:S(2)}) copy-start(bf16[128,3072]{1,0:T(8,128)(2,1)} %get-tuple-element.49) | copy-start | bytes 2359300
  219.8 5.7 %copy-start.2 = (bf16[256,1024]{1,0:T(8,128)(2,1)S(1)}, bf16[256,1024]{1,0:T(8,128)(2,1)}, u32[]{:S(2)}) copy-start(bf16[256,1024]{1,0:T(8,128)(2,1)} %get-tuple-element.46) | copy-start | bytes 1572868
  222.6 4.0 %copy-start.5 = (bf16[128,1024]{1,0:T(8,128)(2,1)S(1)}, bf16[128,1024]{1,0:T(8,128)(2,1)}, u32[]{:S(2)}) copy-start(bf16[128,1024]{1,0:T(8,128)(2,1)} %get-tuple-element.50) | copy-start | bytes 786436
  222.6 4.8 %copy-start.6 = (bf16[128,1024]{1,0:T(8,128)(2,1)S(1)}, bf16[128,1024]{1,0:T(8,128)(2,1)}, u32[]{:S(2)}) copy-start(bf16[128,1024]{1,0:T(8,128)(2,1)} %get-tuple-element.43) | copy-start | bytes 786436
  222.7 5.5 %copy-start.4 = (f32[128,1024]{1,0:T(8,128)S(1)}, f32[128,1024]{1,0:T(8,128)}, u32[]{:S(2)}) copy-start(f32[128,1024]{1,0:T(8,128)} %get-tuple-element.44) | copy-start | bytes 1572868
  222.7 6.3 %copy-start.3 = (f32[128,1024]{1,0:T(8,128)S(1)}, f32[128,1024]{1,0:T(8,128)}, u32[]{:S(2)}) copy-start(f32[128,1024]{1,0:T(8,128)} %get-tuple-element.45) | copy-start | bytes 1572868

commit v2 on v0

--- a/solution.py
+++ b/solution.py
@@ -3,6 +3,8 @@
 import jax
 import jax.numpy as jnp
 from jax import lax
+from jax.experimental import pallas as pl
+from jax.experimental.pallas import tpu as pltpu
 from jax.sharding import PartitionSpec as P
 
 HEADS = 16
@@ -403,6 +405,879 @@
     )
 
 
+RELATIVE = (0, 6, 2, 4, 1, 7, 3, 5)
+PAIRS = (0, 3, 1, 2)
+MESH = pl.DeviceIdType.MESH
+MIB = 2**20
+FAR_FIRST = (4, 5, 2, 3, 6, 7, 1)
+GROUP = ((2, 0), (0, 1), (2, 1), (3, 0), (3, 1), (1, 1), (1, 0))
+ROOT = math.sqrt(2.0 / math.pi)
+
+
+def bit(value, place):
+    return lax.rem(lax.div(value, jnp.int32(1 << place)), jnp.int32(2))
+
+
+def flip(value, mask):
+    out = value
+    for place in range(3):
+        if (mask >> place) & 1:
+            out = out + (1 << place) * (1 - 2 * bit(value, place))
+    return out
+
+
+def exclusive(value, other):
+    return sum(
+        (1 << place) * lax.rem(bit(value, place) + bit(other, place), jnp.int32(2))
+        for place in range(3)
+    )
+
+
+def columns(start, size):
+    return pl.ds(pl.multiple_of(start, 128), size)
+
+
+class Links:
+    def __init__(self, send_sems, recv_sems, load_sems):
+        self.send_sems, self.recv_sems, self.load_sems = send_sems, recv_sems, load_sems
+        self.used, self.loads, self.sent = 0, 0, []
+        self.dp_index, self.seq_index = lax.axis_index("dp"), lax.axis_index("seq")
+
+    def peer(self, dp_mask, seq_mask):
+        return (flip(self.dp_index, dp_mask), flip(self.seq_index, seq_mask))
+
+    def barrier(self):
+        semaphore = pltpu.get_barrier_semaphore()
+        masks = [(0, mask) for mask in range(2, 8)] + list(GROUP)
+        for mask in masks:
+            pl.semaphore_signal(
+                semaphore, inc=1, device_id=self.peer(*mask), device_id_type=MESH
+            )
+        return lambda: pl.semaphore_wait(semaphore, len(masks))
+
+    def send(self, source, target, dp_mask, seq_mask):
+        number = self.used
+        self.used += 1
+        copy = pltpu.make_async_remote_copy(
+            src_ref=source,
+            dst_ref=target,
+            send_sem=self.send_sems.at[number],
+            recv_sem=self.recv_sems.at[number],
+            device_id=self.peer(dp_mask, seq_mask),
+            device_id_type=MESH,
+        )
+        copy.start()
+        self.sent.append(copy)
+        return copy
+
+    def load(self, source, target):
+        copy = pltpu.make_async_copy(source, target, self.load_sems.at[self.loads])
+        self.loads += 1
+        copy.start()
+        return copy
+
+    def settle(self, copy):
+        copy.wait()
+        self.sent = [other for other in self.sent if other is not copy]
+
+    def sent_done(self, copies):
+        for copy in copies:
+            copy.wait_send()
+        self.sent = [other for other in self.sent if not any(other is copy for copy in copies)]
+
+    def drain(self):
+        for copy in self.sent:
+            copy.wait_send()
+
+
+class Share:
+    def __init__(self, links, slots, near, far):
+        self.links, self.slots = links, slots
+        self.across = links.send(near, slots.at[2], 2, 0)
+        self.beside = links.send(far, slots.at[4], 0, 1)
+        self.corner = links.send(far, slots.at[6], 2, 1)
+        self.waits = [links.send(near, slots.at[1], 1, 0)]
+
+    def forward(self):
+        for copy, slot in ((self.across, 2), (self.beside, 4), (self.corner, 6)):
+            copy.wait_recv()
+            self.waits.append(
+                self.links.send(self.slots.at[slot], self.slots.at[slot + 1], 1, 0)
+            )
+
+    def wait(self):
+        arrived(self.waits)
+
+
+def arrived(copies):
+    for copy in copies:
+        copy.wait_recv()
+
+
+def turn_sine_cosine(angles):
+    turns = jnp.floor(angles * (0.5 / math.pi) + 0.5)
+    rest = angles - turns * 6.28125
+    rest = rest - turns * (2.0 * math.pi - 6.28125)
+    return jnp.sin(rest), jnp.cos(rest)
+
+
+def utterance_ends(lengths_ref):
+    ends, total = [], jnp.int32(0)
+    for number in range(lengths_ref.shape[1]):
+        total = total + lengths_ref[0, number]
+        ends.append(total)
+    return ends
+
+
+def segments(ends, index):
+    return sum((index >= end).astype(jnp.int32) for end in ends)
+
+
+def rotary(ends, first_row, rows, width):
+    index = first_row + lax.broadcasted_iota(jnp.int32, (rows, width), 0)
+    start = jnp.zeros_like(index)
+    for end in ends:
+        start = jnp.where(index >= end, end, start)
+    lane = lax.broadcasted_iota(jnp.int32, (rows, width), 1) % HEAD
+    pair = (lane % (HEAD // 2)).astype(jnp.float32)
+    angles = (index - start).astype(jnp.float32) * jnp.exp(
+        pair * (-2.0 * math.log(10000.0) / HEAD)
+    )
+    sine, cosine = turn_sine_cosine(angles)
+    return cosine, jnp.where(lane < HEAD // 2, -sine, sine)
+
+
+def partner(values):
+    half_size = HEAD // 2
+    lane = lax.broadcasted_iota(jnp.int32, values.shape, 1) % HEAD
+    return jnp.where(
+        lane < half_size,
+        pltpu.roll(values, values.shape[1] - half_size, 1),
+        pltpu.roll(values, half_size, 1),
+    )
+
+
+def head_mask(values, head):
+    lane = lax.broadcasted_iota(jnp.int32, values.shape, 1)
+    return jnp.where(lane // HEAD == head, values, jnp.zeros_like(values))
+
+
+def norm_parts(values):
+    centered = values - jnp.mean(values, axis=-1, keepdims=True)
+    variance = jnp.mean(centered * centered, axis=-1, keepdims=True)
+    factor = lax.rsqrt(variance + 1e-06)
+    return centered * factor, factor
+
+
+def norm_back(grad, normal, factor):
+    mean_grad = jnp.mean(grad, axis=-1, keepdims=True)
+    mean_product = jnp.mean(grad * normal, axis=-1, keepdims=True)
+    return factor * (grad - mean_grad - normal * mean_product)
+
+
+def product(left, right):
+    return jnp.dot(left, right, preferred_element_type=jnp.float32)
+
+
+def product_cols(left, right):
+    return lax.dot_general(left, right, contract_cols, preferred_element_type=jnp.float32)
+
+
+def product_rows(left, right):
+    return lax.dot_general(left, right, contract_rows, preferred_element_type=jnp.float32)
+
+
+def gelu_parts(upper):
+    square = upper * upper
+    bent = jnp.tanh(ROOT * (upper + 0.044715 * upper * square))
+    value = 0.5 * upper * (1.0 + bent)
+    slope = 0.5 * (1.0 + bent) + 0.5 * upper * (1.0 - bent * bent) * ROOT * (
+        1.0 + 3.0 * 0.044715 * square
+    )
+    return value, slope
+
+
+class Sum:
+    def __init__(self, links, left, right, total, into_a, into_b, place=None):
+        self.links, self.left, self.right, self.total = links, left, right, total
+        self.into_a, self.into_b, self.place = into_a, into_b, place
+        self.size = total.shape[0] // 4
+
+    def fill(self, low, high):
+        depth = self.left.shape[0] * self.left.shape[1]
+
+        def step(number, carried):
+            start = pl.multiple_of(number * 256, 256)
+            source = start if self.place is None else self.place(number)
+            self.total[pl.ds(start, 256), :] = product_rows(
+                self.left[:, :, columns(source, 256)].reshape(depth, 256),
+                self.right[...].reshape(depth, self.right.shape[2]),
+            ).astype(jnp.bfloat16)
+            return carried
+
+        lax.fori_loop(low // 256, high // 256, step, 0)
+
+    def begin(self):
+        self.fill(2 * self.size, 4 * self.size)
+        self.copy = self.links.send(self.total.at[2 * self.size :], self.into_a, 0, 2)
+
+    def keep(self):
+        self.fill(0, 2 * self.size)
+
+    def second(self):
+        self.links.settle(self.copy)
+        both = pl.ds(0, 2 * self.size)
+        self.total[both, :] = (
+            self.total[both, :].astype(jnp.float32) + self.into_a[...].astype(jnp.float32)
+        ).astype(jnp.bfloat16)
+        self.copy = self.links.send(
+            self.total.at[self.size : 2 * self.size], self.into_b, 0, 6
+        )
+
+    def third(self):
+        self.copy.wait_recv()
+        self.ready = self.total.at[2 * self.size : 3 * self.size]
+        self.ready[...] = (
+            self.total[: self.size, :].astype(jnp.float32) + self.into_b[...].astype(jnp.float32)
+        ).astype(jnp.bfloat16)
+
+    def gather(self, ready, place):
+        self.target = place
+        own = place(self.links.dp_index)
+        self.across = self.links.send(ready, own, 2, 0)
+        self.core = self.links.send(ready, own, 1, 0)
+        self.own = self.links.load(ready, own)
+
+    def spread(self):
+        self.across.wait_recv()
+        other = self.target(flip(self.links.dp_index, 2))
+        self.far = self.links.send(other, other, 1, 0)
+
+    def finish(self):
+        self.own.wait()
+        arrived([self.core, self.far])
+
+
+def layer_kernel(
+    lengths, steps, frame_mask, frames, skip, cotangent, biases, w_skip, w_ada, w_qkv, w_out, w_up,
+    w_down,
+    result, grad_frames, grad_skip, sum_skip, sum_qkv, sum_out, sum_up, sum_down, small_all,
+    embed_all,
+    out_buf, up_buf, down_buf, weight_buf,
+    joined_all, cot_all, first_all, attn_all, second_all, gated_all, upper_all, branch_all,
+    packed_all, in_all,
+    first_own, embed_own, masks, table, packed_send, packed, attn_send, attn_low,
+    attn_sum, residual, scale, grad_gated, second_low, gated, upper_parts, residual_mid, normal_mid,
+    grad_mid, branch, grad_heads, back_recv, grad_packed, grad_in, key_total,
+    value_total, small, small_send, small_recv, up_ready,
+    down_sum, down_a, down_b, up_sum, up_a, up_b, out_sum, out_a, out_b, qkv_sum, qkv_a, qkv_b,
+    skip_sum, skip_a, skip_b,
+    send_sems, recv_sems, load_sems,
+):
+    links = Links(send_sems, recv_sems, load_sems)
+    seq_index, dp_index = links.seq_index, links.dp_index
+    rows, width = frames.shape
+    hidden = grad_gated.shape[1]
+    float32, bfloat16 = jnp.float32, jnp.bfloat16
+    odd = bit(seq_index, 0)
+    enter = links.barrier()
+    load_skip = links.load(w_skip, down_buf.at[: 2 * width])
+    load_ada = links.load(w_ada, weight_buf)
+    load_qkv = links.load(w_qkv, up_buf.at[:, : 3 * width])
+    load_out = links.load(w_out, out_buf)
+    load_down_high = links.load(w_down.at[2 * width :], down_buf.at[2 * width :])
+
+    def relative(source, target, size):
+        for number, mask in enumerate(RELATIVE):
+            target[:, number * size : (number + 1) * size] = source(flip(seq_index, mask))
+
+    def joined_block(place):
+        inside = columns(lax.rem(place, jnp.int32(4)) * 256, 256)
+        return jnp.where(place < 4, frames[:, inside], skip[:, inside])
+
+    joined_own = grad_packed.at[:, width:]
+    relative(joined_block, joined_own, 256)
+    joined_all[0] = joined_own[:, :width]
+    cot_all[0] = cotangent[...]
+    masks[0] = jnp.broadcast_to(frame_mask[...], masks.shape[1:])
+    ends = utterance_ends(lengths)
+    utter = lax.broadcasted_iota(jnp.int32, embed_own.shape, 0)
+    flow = jnp.zeros(embed_own.shape, float32)
+    for number in range(steps.shape[1]):
+        flow = jnp.where(utter == number, steps[0, number].astype(float32), flow)
+    lane = lax.broadcasted_iota(jnp.int32, embed_own.shape, 1)
+    half = width // 2
+    frequency = jnp.exp((lane % half).astype(float32) * (-math.log(10000.0) / half))
+    sine, cosine = turn_sine_cosine(1000.0 * (flow / TSTEPS) * frequency)
+    embed = jnp.where(lane < half, sine, cosine)
+    embed_own[...] = jnp.where(utter < steps.shape[1], embed, 0.0).astype(bfloat16)
+    enter()
+    mask_copies = [links.send(masks.at[0], masks.at[m], 0, m) for m in range(1, 8)]
+    cot_share = Share(links, cot_all, cot_all.at[0], cot_all.at[0])
+    load_skip.wait()
+    residual[...] = product(frames[...], down_buf[:width]) + product(
+        skip[...], down_buf[width : 2 * width]
+    )
+    load_down_low = links.load(w_down.at[: 2 * width], down_buf.at[: 2 * width])
+    load_ada.wait()
+    table[...] = product(embed_own[...], weight_buf[...]) + biases[:, : 2 * width].astype(float32)
+    first_row = seq_index * rows
+    normal, unused = norm_parts(residual[...])
+    row_index = first_row + lax.broadcasted_iota(jnp.int32, (rows, 1), 0)
+    own_segment = segments(ends, row_index)
+    spread_scale = jnp.zeros((rows, width), float32)
+    spread_shift = jnp.zeros((rows, width), float32)
+    for number in range(len(ends)):
+        member = own_segment == number
+        spread_scale = jnp.where(member, table[number : number + 1, :width], spread_scale)
+        spread_shift = jnp.where(member, table[number : number + 1, width:], spread_shift)
+    scale[...] = spread_scale
+    second_low[...] = (normal * (1.0 + spread_scale) + spread_shift).astype(bfloat16)
+    cos_own, sin_own = rotary(ends, first_row, rows, 256)
+    load_qkv.wait()
+    packed_copies = []
+    for far in (2, 1, 3, 0):
+        pair = flip(lax.div(seq_index, jnp.int32(2)), far)
+        parts = []
+        for kind in range(3):
+            part = product(second_low[...], up_buf[:, columns(kind * width + pair * 256, 256)])
+            if kind < 2:
+                part = part * cos_own + partner(part) * sin_own
+            parts.append(part.astype(bfloat16))
+        for side in range(2):
+            for kind in range(3):
+                packed_send[pair * 2 + side, :, kind * 128 : (kind + 1) * 128] = parts[kind][
+                    :, side * 128 : (side + 1) * 128
+                ]
+        for mask in (2 * far, 2 * far + 1):
+            if mask:
+                packed_copies.append(
+                    links.send(
+                        packed_send.at[flip(seq_index, mask)], packed.at[seq_index], 0, mask
+                    )
+                )
+    packed[seq_index] = packed_send[seq_index]
+    load_up = links.load(w_up, up_buf)
+    relative(lambda place: second_low[:, columns(place * 128, 128)], first_own, 128)
+    first_all[0] = first_own[:, : width // 2]
+    joined_share = Share(links, joined_all, joined_all.at[0], joined_own.at[:, width:])
+    first_share = Share(links, first_all, first_all.at[0], first_own.at[:, width // 2 :])
+    embed_copies = [links.send(embed_own, embed_all.at[dp_index], m, 0) for m in (1, 2, 3)]
+    embed_load = links.load(embed_own, embed_all.at[dp_index])
+    load_down_low.wait()
+    load_down_high.wait()
+
+    def gated_step(step, carried):
+        part = columns(step * 512, 512)
+        grad_gated[:, part] = product_cols(cotangent[...], down_buf[part, :])
+        return carried
+
+    lax.fori_loop(0, hidden // 512, gated_step, 0)
+    cot_share.forward()
+    arrived(mask_copies)
+    arrived(packed_copies)
+    key_index = lax.broadcasted_iota(jnp.int32, (1, 8 * rows), 1)
+    key_segment = segments(ends, key_index)
+    key_valid = jnp.concatenate(
+        [masks[exclusive(seq_index, jnp.int32(number))][:1] for number in range(8)], axis=1
+    )
+
+    def attend(place):
+        query = packed[place, :, :128]
+        row_index = place * rows + lax.broadcasted_iota(jnp.int32, (rows, 1), 0)
+        allowed = (segments(ends, row_index) == key_segment) & (
+            (key_valid > 0) | (row_index == key_index)
+        )
+        keys = packed[:, :, 128:256].reshape(8 * rows, 128)
+        values = packed[:, :, 256:].reshape(8 * rows, 128)
+        total = jnp.zeros((rows, 128), float32)
+        here = pl.ds(pl.multiple_of(place * rows, rows), rows)
+        for head in range(2):
+            scores = product_cols(head_mask(query, head), keys) * (1.0 / math.sqrt(HEAD))
+            scores = jnp.where(allowed, scores, masked_score)
+            raised = jnp.exp(scores - jnp.max(scores, axis=1, keepdims=True))
+            low = (raised / jnp.sum(raised, axis=1, keepdims=True)).astype(bfloat16)
+            weight_buf[here, head * 1024 : (head + 1) * 1024] = low
+            total = total + product(low, head_mask(values, head))
+        attn_sum[here, :] = total
+        attn_send[place] = total.astype(bfloat16)
+
+    base = links.used
+    links.used += 8
+
+    def attn_copy(mask):
+        target = exclusive(seq_index, mask)
+        return pltpu.make_async_remote_copy(
+            src_ref=attn_send.at[target],
+            dst_ref=attn_low.at[seq_index],
+            send_sem=send_sems.at[base + mask],
+            recv_sem=recv_sems.at[base + mask],
+            device_id=(dp_index, target),
+            device_id_type=MESH,
+        )
+
+    def attend_step(step, carried):
+        mask = 7 - step
+        attend(exclusive(seq_index, mask))
+        attn_copy(mask).start()
+        return carried
+
+    lax.fori_loop(0, 7, attend_step, 0)
+    attend(seq_index)
+    attn_low[seq_index] = attn_send[seq_index]
+    joined_share.forward()
+    first_share.forward()
+    load_out.wait()
+    for mask in range(1, 8):
+        attn_copy(jnp.int32(mask)).wait()
+    joined_attn = jnp.concatenate([attn_low[number] for number in range(8)], axis=1)
+    residual_mid[...] = residual[...] + product(joined_attn, out_buf[...])
+    normal, factor_mid = norm_parts(residual_mid[...])
+    normal_mid[...] = normal
+    gain_float = biases[:, 7 * width : 8 * width].astype(float32)
+    second_all[0] = (normal * gain_float).astype(bfloat16)
+    second_share = Share(links, second_all, second_all.at[0], second_all.at[0])
+    small[8:] = jnp.zeros((8, small.shape[1]), float32)
+    load_up.wait()
+
+    def up_step(step, carried):
+        part = columns(step * 512, 512)
+        upper = product(second_all[0], up_buf[:, part]) + biases[
+            :, columns(2 * width + step * 512, 512)
+        ].astype(float32)
+        value, slope = gelu_parts(upper)
+        grad_upper = (grad_gated[:, part] * slope).astype(bfloat16)
+        gated[:, part] = value.astype(bfloat16)
+        upper_parts[:, part] = grad_upper
+        small[
+            pl.ds(8 + lax.div(step, jnp.int32(4)), 1),
+            columns(lax.rem(step, jnp.int32(4)) * 512, 512),
+        ] = jnp.sum(grad_upper.astype(float32), axis=0, keepdims=True)
+        return carried
+
+    lax.fori_loop(0, hidden // 512, up_step, 0)
+
+    def second_step(step, total):
+        part = columns(step * 512, 512)
+        return total + product_cols(upper_parts[:, part], up_buf[:, part])
+
+    grad_second = lax.fori_loop(
+        0, hidden // 512, second_step, jnp.zeros((rows, width), float32)
+    )
+    grad_out = cotangent[...].astype(float32)
+    normal = normal_mid[...]
+    small[10:11, :width] = jnp.sum(grad_second * normal, axis=0, keepdims=True)
+    small[10:11, width:] = jnp.sum(grad_out, axis=0, keepdims=True)
+    grad_mid[...] = grad_out + norm_back(grad_second * gain_float, normal, factor_mid)
+    branch[...] = grad_mid[...].astype(bfloat16)
+    grad_attn = product_cols(branch[...], out_buf[...]).astype(bfloat16)
+    grad_send = attn_send
+    for number in range(8):
+        grad_send[number] = grad_attn[:, number * 128 : (number + 1) * 128]
+    head_copies = [
+        links.send(grad_send.at[flip(seq_index, m)], grad_heads.at[seq_index], 0, m)
+        for m in FAR_FIRST
+    ]
+    grad_heads[seq_index] = grad_send[seq_index]
+
+    def quarters(source, slots):
+        size = slots.shape[2]
+        slots[0] = source[:, columns(dp_index * size, size)]
+        return [
+            links.send(
+                source.at[:, columns(flip(dp_index, m) * size, size)], slots.at[4 * v + m], m, v
+            )
+            for m, v in GROUP
+        ]
+
+    second_share.forward()
+    branch_copies = quarters(branch, branch_all)
+    attn_own = grad_packed.at[:, :width]
+    relative(lambda place: attn_low[place], attn_own, 128)
+    attn_all[0] = attn_own[:, : width // 2]
+    attn_share = Share(links, attn_all, attn_all.at[0], attn_own.at[:, width // 2 :])
+
+    def down_step(step, total):
+        part = columns(step * 512, 512)
+        return total + product(gated[:, part], down_buf[part, :])
+
+    lower = lax.fori_loop(
+        0,
+        hidden // 512,
+        down_step,
+        residual_mid[...] + biases[:, 6 * width : 7 * width].astype(float32),
+    )
+    second_low[...] = lower.astype(bfloat16)
+    out_loads = [links.load(second_low, result)]
+    second_share.wait()
+    cot_share.wait()
+    for first in (0, 2):
+        units, spots = [], []
+        for number in (first, first + 1):
+            place = flip(seq_index, RELATIVE[number])
+            units.append(columns(place * 512 + dp_index * 128, 128))
+            spots.append(lax.div(place, jnp.int32(2)))
+        weight_up = jnp.concatenate([up_buf[:, unit] for unit in units], axis=1)
+        weight_down = jnp.concatenate([down_buf[unit, :] for unit in units], axis=0)
+        bias = jnp.concatenate(
+            [
+                biases[:, columns(2 * width + flip(seq_index, RELATIVE[number]) * 512 + dp_index * 128, 128)]
+                for number in (first, first + 1)
+            ],
+            axis=1,
+        ).astype(float32)
+
+        def again_step(step, carried):
+            both = pl.ds(2 * step, 2)
+            upper = product(second_all[both].reshape(2 * rows, width), weight_up) + bias
+            value, slope = gelu_parts(upper)
+            grad = product_cols(cot_all[both].reshape(2 * rows, width), weight_down)
+            gated_all[both, :, first * 128 : (first + 2) * 128] = value.astype(bfloat16).reshape(
+                2, rows, 256
+            )
+            grad_upper = (grad * slope).astype(bfloat16).reshape(2, rows, 256)
+            for side in range(2):
+                upper_all[both, :, columns(spots[side] * 128, 128)] = grad_upper[
+                    :, :, side * 128 : (side + 1) * 128
+                ]
+            return carried
+
+        lax.fori_loop(0, 4, again_step, 0)
+    load_qkv = links.load(w_qkv, up_buf.at[:, : 3 * width])
+    load_skip = links.load(w_skip, down_buf.at[: 2 * width])
+
+    def pair_place(number):
+        base_pair = lax.div(seq_index, jnp.int32(2))
+        step_a, step_b = lax.div(number, jnp.int32(2)), lax.rem(number, jnp.int32(2))
+        two = jnp.int32(2)
+        low_bit = lax.rem(bit(base_pair, 0) + step_a + step_b, two)
+        high_bit = lax.rem(bit(base_pair, 1) + step_b, two)
+        return (2 * high_bit + low_bit) * 256
+
+    down = Sum(links, gated_all, cot_all, down_sum, down_a, down_b)
+    up = Sum(links, second_all, upper_all, up_sum, up_a, up_b, pair_place)
+    out = Sum(links, attn_all, branch_all, out_sum, out_a, out_b)
+    qkv = Sum(links, first_all, packed_all, qkv_sum, qkv_a, qkv_b)
+    skip_in = Sum(links, joined_all, in_all, skip_sum, skip_a, skip_b)
+    down.begin()
+    up.begin()
+    arrived(head_copies)
+    links.sent_done(packed_copies)
+    back_send = packed_send
+    shrink = 1.0 / math.sqrt(HEAD)
+    key_total[...] = jnp.zeros_like(key_total)
+    value_total[...] = jnp.zeros_like(value_total)
+
+    def back_step(place, carried):
+        here = pl.ds(pl.multiple_of(place * rows, rows), rows)
+        grad = grad_heads[place]
+        query = packed[place, :, :128]
+        keys = packed[:, :, 128:256].reshape(8 * rows, 128)
+        values = packed[:, :, 256:].reshape(8 * rows, 128)
+        both = grad.astype(float32) * attn_sum[here, :]
+        total = jnp.zeros((rows, 128), float32)
+        for head in range(2):
+            low = weight_buf[here, head * 1024 : (head + 1) * 1024]
+            grad_head = head_mask(grad, head)
+            delta = jnp.sum(head_mask(both, head), axis=1, keepdims=True)
+            grad_scores = (
+                low.astype(float32) * (product_cols(grad_head, values) - delta)
+            ).astype(bfloat16)
+            total = total + product(grad_scores, head_mask(keys, head))
+            key_total[...] += product_rows(grad_scores, head_mask(query, head))
+            value_total[...] += product_rows(low, grad_head)
+        total = total * shrink
+        cosine, sine = rotary(ends, place * rows, rows, 128)
+        back_send[place, :, :128] = (total * cosine - partner(total) * sine).astype(bfloat16)
+        return carried
+
+    lax.fori_loop(0, 8, back_step, 0)
+
+    def key_step(place, carried):
+        here = pl.ds(pl.multiple_of(place * rows, rows), rows)
+        total = key_total[here, :] * shrink
+        cosine, sine = rotary(ends, place * rows, rows, 128)
+        back_send[place, :, 128:256] = (total * cosine - partner(total) * sine).astype(bfloat16)
+        back_send[place, :, 256:] = value_total[here, :].astype(bfloat16)
+        return carried
+
+    lax.fori_loop(0, 8, key_step, 0)
+    back_copies = [
+        links.send(back_send.at[flip(seq_index, m)], back_recv.at[seq_index], 0, m)
+        for m in FAR_FIRST
+    ]
+    back_recv[seq_index] = back_send[seq_index]
+    down.keep()
+    up.keep()
+    attn_share.forward()
+    arrived(branch_copies)
+    attn_share.wait()
+    out.begin()
+    out.keep()
+    arrived(back_copies)
+    for share in (joined_share, attn_share):
+        links.sent_done([share.beside, share.corner])
+    for number in range(8):
+        for kind in range(3):
+            grad_packed[:, kind * width + number * 128 : kind * width + (number + 1) * 128] = (
+                back_recv[number, :, kind * 128 : (kind + 1) * 128]
+            )
+    packed_copies = quarters(grad_packed, packed_all)
+    load_qkv.wait()
+
+    def first_step(step, total):
+        part = columns(step * 512, 512)
+        return total + product_cols(grad_packed[:, part], up_buf[:, part])
+
+    grad_first = lax.fori_loop(0, 6, first_step, jnp.zeros((rows, width), float32))
+    normal, factor = norm_parts(residual[...])
+    grad_in[...] = (
+        grad_mid[...] + norm_back(grad_first * (1.0 + scale[...]), normal, factor)
+    ).astype(bfloat16)
+    in_copies = quarters(grad_in, in_all)
+    scaled = grad_first * normal
+    for number in range(len(ends)):
+        member = own_segment == number
+        small[number : number + 1, :width] = jnp.sum(
+            jnp.where(member, scaled, 0.0), axis=0, keepdims=True
+        )
+        small[number : number + 1, width:] = jnp.sum(
+            jnp.where(member, grad_first, 0.0), axis=0, keepdims=True
+        )
+
+    def small_start(number, mask):
+        small_send[number] = small[...].astype(bfloat16)
+        return links.send(small_send.at[number], small_recv.at[number], 0, mask)
+
+    def small_add(copy, number):
+        copy.wait_recv()
+        small[...] = small_send[number].astype(float32) + small_recv[number].astype(float32)
+
+    small_copy = small_start(0, 1)
+    down.second()
+    up.second()
+    first_share.wait()
+    arrived(packed_copies)
+    qkv.begin()
+    joined_share.wait()
+    arrived(in_copies)
+    skip_in.begin()
+    small_add(small_copy, 0)
+    small_copy = small_start(1, 2)
+    out.second()
+    qkv.keep()
+    skip_in.keep()
+    load_skip.wait()
+    for held, target, start in ((residual, grad_frames, 0), (normal_mid, grad_skip, width)):
+        held[...] = product_cols(grad_in[...], down_buf[start : start + width, :])
+        out_loads.append(links.load(held, target))
+    by_rows = lambda target, size: lambda index: target.at[pl.ds(index * size, size), :]
+    by_cols = lambda target, size: lambda index: target.at[:, columns(index * size, size)]
+    down.third()
+    down.gather(down.ready, by_rows(sum_down, 128))
+    up.third()
+    up_ready[odd] = up.ready[pl.ds(pl.multiple_of(odd * 128, 128), 128), :]
+    up_other = links.send(
+        up.ready.at[pl.ds(pl.multiple_of((1 - odd) * 128, 128), 128), :], up_ready.at[odd], 0, 1
+    )
+    small_add(small_copy, 1)
+    small_copy = small_start(2, 6)
+    out.third()
+    out.gather(out.ready, by_cols(sum_out, 256))
+    up_other.wait_recv()
+    up.gather(up_ready, lambda index: sum_up.at[index])
+    qkv.second()
+    skip_in.second()
+    small_add(small_copy, 2)
+    small_send[3] = small[...].astype(bfloat16)
+    small_copies = [
+        links.send(small_send.at[3], small_all.at[dp_index], m, 0) for m in (3, 2, 1)
+    ]
+    small_load = links.load(small_send.at[3], small_all.at[dp_index])
+    down.spread()
+    out.spread()
+    up.spread()
+    qkv.third()
+    qkv.gather(qkv.ready, by_cols(sum_qkv, 768))
+    skip_in.third()
+    skip_in.gather(skip_in.ready, by_cols(sum_skip, 256))
+    qkv.spread()
+    skip_in.spread()
+    small_load.wait()
+    embed_load.wait()
+    for load in out_loads:
+        load.wait()
+    arrived(small_copies + embed_copies)
+    for each in (down, up, out, qkv, skip_in):
+        each.finish()
+    links.drain()
+
+
+def widen_kernel(
+    result_in, frames_in, skip_in, sum_skip, sum_qkv, sum_out, sum_up, sum_down, small_all, embed_all,
+    result, grad_frames, grad_skip, out_skip, out_ada, out_ada_bias, out_qkv, out_out, out_gain,
+    out_up, out_up_bias, out_down, out_down_bias,
+    low_result, low_frames, low_skip, low_w_skip, low_qkv, low_out, low_up, low_down, low_small, low_embed,
+    full_skip, full_ada, full_qkv, full_out, full_up, full_down, in_sems, out_sems,
+):
+    float32 = jnp.float32
+    seq_index = lax.axis_index("seq")
+    sources = (sum_up, sum_down, sum_qkv, sum_skip, small_all, embed_all, sum_out, result_in, frames_in, skip_in)
+    inside = (low_up, low_down, low_qkv, low_w_skip, low_small, low_embed, low_out, low_result, low_frames, low_skip)
+    loads = [
+        pltpu.make_async_copy(source, target, in_sems.at[number])
+        for number, (source, target) in enumerate(zip(sources, inside, strict=True))
+    ]
+    for load in loads:
+        load.start()
+    stores = []
+
+    def store(source, target):
+        copy = pltpu.make_async_copy(source, target, out_sems.at[len(stores)])
+        copy.start()
+        stores.append(copy)
+
+    loads[0].wait()
+    for quarter in range(4):
+        for side in range(2):
+            for level in range(4):
+                start = (2 * level + side) * 512 + quarter * 128
+                full_up[:, start : start + 128] = low_up[
+                    quarter, side, :, level * 128 : (level + 1) * 128
+                ].astype(float32)
+    store(full_up, out_up)
+    for number, low, full, out in (
+        (1, low_down, full_down, out_down),
+        (2, low_qkv, full_qkv, out_qkv),
+        (3, low_w_skip, full_skip, out_skip),
+    ):
+        loads[number].wait()
+        full[...] = low[...].astype(float32)
+        store(full, out)
+    loads[4].wait()
+    loads[5].wait()
+    size = full_ada.shape[0]
+    own = low_embed[:, :, columns(seq_index * size, size)].reshape(-1, size)
+    full_ada[...] = product_rows(own, low_small[...].reshape(own.shape[0], full_ada.shape[1]))
+    store(full_ada, out_ada)
+    loads[6].wait()
+    full_out[...] = low_out[...].astype(float32)
+    store(full_out, out_out)
+    for number, low, out in ((7, low_result, result), (8, low_frames, grad_frames), (9, low_skip, grad_skip)):
+        loads[number].wait()
+        store(low, out)
+    wide = low_small.shape[2]
+    spot = columns(seq_index * 256, 256)
+    bias = jnp.zeros((1, 256), float32)
+    for number in range(4):
+        bias = bias + jnp.sum(low_small[number, :8, spot].astype(float32), axis=0, keepdims=True)
+    out_ada_bias[...] = bias
+    upper = jnp.zeros((1, 512), float32)
+    gain = jnp.zeros((1, 128), float32)
+    down_bias = jnp.zeros((1, 128), float32)
+    high = lax.div(seq_index, jnp.int32(4))
+    for number in range(4):
+        both = low_small[number, 8:, columns(lax.rem(seq_index, jnp.int32(4)) * 512, 512)].astype(float32)
+        upper = upper + jnp.where(high == 0, both[:1], both[1:2])
+        gain = gain + low_small[number, 8:, columns(seq_index * 128, 128)].astype(float32)[2:3]
+        down_bias = down_bias + low_small[number, 8:, columns(wide // 2 + seq_index * 128, 128)].astype(float32)[2:3]
+    out_up_bias[...] = upper
+    out_gain[...] = gain
+    out_down_bias[...] = down_bias
+    for copy in stores:
+        copy.wait()
+
+
+def one_kernel(
+    frames, skip, lengths, frame_mask, time_step, w_skip, w_ada, b_ada, w_qkv, w_out, norm_gain,
+    w_up, b_up, w_down, b_down, cotangent,
+):
+    rows, width = frames.shape[1:]
+    hidden = b_up.shape[0]
+    float32, bfloat16 = jnp.float32, jnp.bfloat16
+    shape = jax.ShapeDtypeStruct
+    vmem = pl.BlockSpec(memory_space=pltpu.VMEM)
+    smem = pl.BlockSpec(memory_space=pltpu.SMEM)
+    anywhere = pl.BlockSpec(memory_space=pl.ANY)
+    dma = pltpu.SemaphoreType.DMA
+    low = lambda *size: pltpu.VMEM(size, bfloat16)
+    full = lambda *size: pltpu.VMEM(size, float32)
+    biases = jnp.concatenate([b_ada, b_up, b_down, norm_gain])[None]
+    sums = ((512, 1024), (1024, 512), (512, 256), (512, 768), (1024, 256))
+    sum_scratch = [low(tall // part, wide) for tall, wide in sums for part in (1, 2, 4)]
+    outs = (
+        (shape((rows, width), bfloat16), anywhere),
+        (shape((rows, width), float32), anywhere),
+        (shape((rows, width), float32), anywhere),
+        (shape((2 * width // 8, width), bfloat16), anywhere),
+        (shape((width // 8, 3 * width), bfloat16), anywhere),
+        (shape((width // 8, width), bfloat16), anywhere),
+        (shape((4, 2, width // 8, hidden // 8), bfloat16), anywhere),
+        (shape((hidden // 8, width), bfloat16), anywhere),
+        (shape((4, 16, 2 * width), bfloat16), anywhere),
+        (shape((4, 16, width), bfloat16), anywhere),
+    )
+    parts = pl.pallas_call(
+        layer_kernel,
+        out_shape=tuple(item[0] for item in outs),
+        in_specs=[smem, smem] + [vmem] * 5 + [anywhere] * 6,
+        out_specs=tuple(item[1] for item in outs),
+        scratch_shapes=[
+            low(*w_out.shape), low(*w_up.shape), low(*w_down.shape), low(8 * rows, 2 * width),
+            low(8, rows, width), low(8, rows, width), low(8, rows, width // 2), low(8, rows, width // 2),
+            low(8, rows, width), low(8, rows, 512), low(8, rows, 512), low(8, rows, 256),
+            low(8, rows, 768), low(8, rows, 256),
+            low(rows, width), low(16, width), pltpu.VMEM((8, 8, rows), jnp.int32),
+            full(16, 2 * width), low(8, rows, 384), low(8, rows, 384), low(8, rows, 128), low(8, rows, 128),
+            full(8 * rows, 128), full(rows, width), full(rows, width), full(rows, hidden), low(rows, width),
+            low(rows, hidden), low(rows, hidden), full(rows, width), full(rows, width),
+            full(rows, width), low(rows, width), low(8, rows, 128), low(8, rows, 384), low(rows, 3 * width), low(rows, width), full(8 * rows, 128),
+            full(8 * rows, 128), full(16, 2 * width), low(4, 16, 2 * width), low(3, 16, 2 * width),
+            low(2, rows, 512),
+            *sum_scratch,
+            dma((128,)), dma((128,)), dma((24,)),
+        ],
+        compiler_params=pltpu.CompilerParams(
+            collective_id=0, has_side_effects=True, vmem_limit_bytes=60 * MIB
+        ),
+        name="layer",
+    )(
+        lengths, time_step, frame_mask, frames[0], skip[0], cotangent[0], biases, w_skip, w_ada,
+        w_qkv, w_out, w_up, w_down,
+    )
+
+    last_outs = (
+        (shape((rows, width), bfloat16), anywhere),
+        (shape((rows, width), float32), anywhere),
+        (shape((rows, width), float32), anywhere),
+        (shape((2 * width // 8, width), float32), anywhere),
+        (shape((width // 8, 2 * width), float32), anywhere),
+        (shape((1, 2 * width // 8), float32), vmem),
+        (shape((width // 8, 3 * width), float32), anywhere),
+        (shape((width // 8, width), float32), anywhere),
+        (shape((1, width // 8), float32), vmem),
+        (shape((width // 8, hidden), float32), anywhere),
+        (shape((1, hidden // 8), float32), vmem),
+        (shape((hidden // 8, width), float32), anywhere),
+        (shape((1, width // 8), float32), vmem),
+    )
+    scratch = [pltpu.VMEM(item[0].shape, item[0].dtype) for item in outs]
+    scratch += [full(*last_outs[number][0].shape) for number in (3, 4, 6, 7, 9, 11)]
+    widened = pl.pallas_call(
+        widen_kernel,
+        out_shape=tuple(item[0] for item in last_outs),
+        in_specs=[pl.BlockSpec(memory_space=pltpu.HBM)] * len(outs),
+        out_specs=tuple(item[1] for item in last_outs),
+        scratch_shapes=[*scratch, dma((10,)), dma((12,))],
+        compiler_params=pltpu.CompilerParams(vmem_limit_bytes=40 * MIB),
+        name="widen",
+    )(*parts)
+    return tuple(
+        item[None] if number < 3 else item.reshape(-1) if item.shape[0] == 1 else item
+        for number, item in enumerate(widened)
+    )
+
+
 def solution(mesh):
     placed = (
         P("dp", "seq", None),
@@ -422,8 +1297,9 @@
         P(),
         P("dp", "seq", None),
     )
+    split_heads = mesh.shape["dp"] == 4 and mesh.shape["seq"] == len(RELATIVE)
     return jax.shard_map(
-        on_device,
+        one_kernel if split_heads else on_device,
         mesh=mesh,
         in_specs=placed,
         out_specs=(

time: 1640 us -> 191 us (0.12)
  waiting for transfers between devices: 1380 us -> 0 us
  Pallas kernels: 0 us -> 176 us
  matrix products: 103 us -> 0 us
  blocking collectives: 63.5 us -> 0 us
  other arithmetic: 41.8 us -> 0.74 us
    reduce_scatter x8 -> x0, waiting for transfers between devices: 1280 us -> none  [the longest x1 284 us: on_device(): lax.psum_scatter(grad_up, 'seq', scatter_dimension=0, tiled=True)]
    pallas_call x0 -> x2, Pallas kernels: none -> 176 us  [the longest x1 171 us: one_kernel(): pl.pallas_call(layer_kernel, out_shape=tuple((item[0] for item in outs)),...]
    dot_general x25 -> x0, matrix products: 103 us -> none  [the longest x1 8.35 us: on_device(): lax.dot_general(second_low, grad_upper, contract_rows, preferred_element_...]
    all_gather x2 -> x0, waiting for transfers between devices: 70.6 us -> none  [the longest x1 42.9 us: on_device(): lax.all_gather(values_low, 'seq', axis=0, tiled=True)]
    unnamed x1 -> x0, blocking collectives: 35.2 us -> none
    psum x1 -> x0, waiting for transfers between devices: 30.8 us -> none  [on_device(): lax.psum(share_skip.astype(jnp.bfloat16), 'dp').astype(jnp.float32)]
    convert_element_type x24 -> x0, other arithmetic: 28.6 us -> none  [the longest x1 2.72 us: on_device(): share_down.astype(jnp.bfloat16)]
    all_gather x1 -> x0, blocking collectives: 22.7 us -> none  [on_device(): lax.all_gather(valid_low, 'seq', axis=0, tiled=True)]
  transfers between devices with their start and end apart: 11 -> 0, of which waited for: 11 -> 0; matrix products, arithmetic and copies ran while one was open for 6% -> 0% of each run, Pallas kernels for 0% -> 0%
where the time goes in v2:
time: 191 us; the launch traced here: 189 us
  Pallas kernels  176 us (92%)
  local copies, waits for them, and re-layouts  11.1 us (6%)
    pallas_call x1, Pallas kernels, one_kernel(): pl.pallas_call(layer_kernel, out_shape=tuple((item[0] for item in outs)),...  171 us
    unnamed x20, local copies, waits for them, and re-layouts  10.4 us
    pallas_call x1, Pallas kernels, one_kernel(): pl.pallas_call(widen_kernel, out_shape=tuple((item[0] for item in last_ou...  5.25 us

profile of v2, /device:TPU:0, one launch (start us, length us, event | category | flops | bytes accessed | tf_op | source)
XLA Modules:
  0.0 188.8 jit_solution(1604553603765311103)
XLA Ops:
  0.6 0.7 pad_maximum_fusion
  1.4 0.6 broadcast_in_dim.12.biases
  2.0 170.9 %layer.1 = (bf16[128,1024]{1,0:T(8,128)(2,1)}, f32[128,1024]{1,0:T(8,128)}, f32[128,1024]{1,0:T(8,128)}, bf16[256,1024]{1,0:T(8,128)(2,1)}, bf16[128,3072]{1,0:T...) custom-call(s32[1,8]{1,0:T(1,128)} %lengths.1, ...), custom_call_target="tpu_custom_call" | custom-call | tf_op jit(solution)/shard_map/layer/pallas_call | solution.py:1220
  172.9 0.0 copy-start
  172.9 1.2 copy-done
  174.1 0.0 copy-start.1
  174.2 1.2 copy-done.1
  175.4 0.0 copy-start.2
  175.4 1.1 copy-done.2
  176.5 0.0 copy-start.3
  176.5 1.0 copy-done.3
  177.6 0.0 copy-start.4
  177.6 1.0 copy-done.4
  178.6 0.0 copy-start.5
  178.6 1.0 copy-done.5
  179.6 0.0 copy-start.6
  179.6 0.9 copy-done.6
  180.6 0.0 copy-start.7
  180.6 0.9 copy-done.7
  181.5 0.0 copy-start.8
  181.5 0.9 copy-done.8
  182.5 0.0 copy-start.9
  182.5 0.9 copy-done.9
  183.4 5.2 %widen.1 = (bf16[128,1024]{1,0:T(8,128)(2,1)}, f32[128,1024]{1,0:T(8,128)}, f32[128,1024]{1,0:T(8,128)}, f32[256,1024]{1,0:T(8,128)}, f32[128,2048]{1,0:T(8,128)...) custom-call(bf16[128,1024]{1,0:T(8,128)(2,1)S(1)} %copy-done.6, ...), custom_call_target="tpu_custom_call" | custom-call | tf_op jit(solution)/shard_map/widen/pallas_call | solution.py:1266
Async XLA Ops:
  172.9 1.2 copy-start
  174.1 1.2 copy-start.1
  175.4 1.1 copy-start.2
  176.5 1.0 copy-start.3
  177.6 1.0 copy-start.4
  178.6 1.0 copy-start.5
  179.6 0.9 copy-start.6
  180.6 0.9 copy-start.7
  181.5 0.9 copy-start.8
  182.5 0.9 copy-start.9

commit v3 on v2

--- a/solution.py
+++ b/solution.py
@@ -659,19 +659,20 @@
 
 
 def layer_kernel(
-    lengths, steps, frame_mask, frames, skip, cotangent, biases, w_skip, w_ada, w_qkv, w_out, w_up,
-    w_down,
+    lengths, steps, mask_in, frames_in, skip_frames_in, cot_in, bias_in, w_skip, w_ada, w_qkv, w_out,
+    w_up, w_down,
     result, grad_frames, grad_skip, sum_skip, sum_qkv, sum_out, sum_up, sum_down, small_all,
     embed_all,
     out_buf, up_buf, down_buf, weight_buf,
     joined_all, cot_all, first_all, attn_all, second_all, gated_all, upper_all, branch_all,
     packed_all, in_all,
+    frames, skip, frame_mask, biases,
     first_own, embed_own, masks, table, packed_send, packed, attn_send, attn_low,
     attn_sum, residual, scale, grad_gated, second_low, gated, upper_parts, residual_mid, normal_mid,
-    grad_mid, branch, grad_heads, back_recv, grad_packed, grad_in, key_total,
+    grad_mid, branch, grad_heads, query_recv, pair_recv, grad_packed, grad_in, key_total,
     value_total, small, small_send, small_recv, up_ready,
-    down_sum, down_a, down_b, up_sum, up_a, up_b, out_sum, out_a, out_b, qkv_sum, qkv_a, qkv_b,
-    skip_sum, skip_a, skip_b,
+    down_sum, down_a, down_b, up_sum, up_a, up_b, out_sum, out_a, out_b, skip_sum, skip_a, skip_b,
+    query_sum, query_a, query_b, key_sum, key_a, key_b, value_sum, value_a, value_b,
     send_sems, recv_sems, load_sems,
 ):
     links = Links(send_sems, recv_sems, load_sems)
@@ -680,12 +681,16 @@
     hidden = grad_gated.shape[1]
     float32, bfloat16 = jnp.float32, jnp.bfloat16
     odd = bit(seq_index, 0)
-    enter = links.barrier()
+    load_frames = links.load(frames_in, frames)
+    load_skip_frames = links.load(skip_frames_in, skip)
+    load_mask = links.load(mask_in, frame_mask)
+    load_bias = links.load(bias_in, biases)
     load_skip = links.load(w_skip, down_buf.at[: 2 * width])
     load_ada = links.load(w_ada, weight_buf)
+    enter = links.barrier()
     load_qkv = links.load(w_qkv, up_buf.at[:, : 3 * width])
-    load_out = links.load(w_out, out_buf)
-    load_down_high = links.load(w_down.at[2 * width :], down_buf.at[2 * width :])
+    load_cot = links.load(cot_in, cot_all.at[0])
+    cotangent = cot_all.at[0]
 
     def relative(source, target, size):
         for number, mask in enumerate(RELATIVE):
@@ -695,11 +700,6 @@
         inside = columns(lax.rem(place, jnp.int32(4)) * 256, 256)
         return jnp.where(place < 4, frames[:, inside], skip[:, inside])
 
-    joined_own = grad_packed.at[:, width:]
-    relative(joined_block, joined_own, 256)
-    joined_all[0] = joined_own[:, :width]
-    cot_all[0] = cotangent[...]
-    masks[0] = jnp.broadcast_to(frame_mask[...], masks.shape[1:])
     ends = utterance_ends(lengths)
     utter = lax.broadcasted_iota(jnp.int32, embed_own.shape, 0)
     flow = jnp.zeros(embed_own.shape, float32)
@@ -711,17 +711,19 @@
     sine, cosine = turn_sine_cosine(1000.0 * (flow / TSTEPS) * frequency)
     embed = jnp.where(lane < half, sine, cosine)
     embed_own[...] = jnp.where(utter < steps.shape[1], embed, 0.0).astype(bfloat16)
-    enter()
-    mask_copies = [links.send(masks.at[0], masks.at[m], 0, m) for m in range(1, 8)]
-    cot_share = Share(links, cot_all, cot_all.at[0], cot_all.at[0])
+    first_row = seq_index * rows
+    cos_own, sin_own = rotary(ends, first_row, rows, 256)
+    load_frames.wait()
+    load_skip_frames.wait()
+    load_mask.wait()
+    load_bias.wait()
+    masks[0] = jnp.broadcast_to(frame_mask[...], masks.shape[1:])
     load_skip.wait()
     residual[...] = product(frames[...], down_buf[:width]) + product(
         skip[...], down_buf[width : 2 * width]
     )
-    load_down_low = links.load(w_down.at[: 2 * width], down_buf.at[: 2 * width])
     load_ada.wait()
     table[...] = product(embed_own[...], weight_buf[...]) + biases[:, : 2 * width].astype(float32)
-    first_row = seq_index * rows
     normal, unused = norm_parts(residual[...])
     row_index = first_row + lax.broadcasted_iota(jnp.int32, (rows, 1), 0)
     own_segment = segments(ends, row_index)
@@ -733,7 +735,8 @@
         spread_shift = jnp.where(member, table[number : number + 1, width:], spread_shift)
     scale[...] = spread_scale
     second_low[...] = (normal * (1.0 + spread_scale) + spread_shift).astype(bfloat16)
-    cos_own, sin_own = rotary(ends, first_row, rows, 256)
+    enter()
+    mask_copies = [links.send(masks.at[0], masks.at[m], 0, m) for m in range(1, 8)]
     load_qkv.wait()
     packed_copies = []
     for far in (2, 1, 3, 0):
@@ -756,8 +759,16 @@
                         packed_send.at[flip(seq_index, mask)], packed.at[seq_index], 0, mask
                     )
                 )
+    load_down_low = links.load(w_down.at[: 2 * width], down_buf.at[: 2 * width])
+    load_down_high = links.load(w_down.at[2 * width :], down_buf.at[2 * width :])
+    load_out = links.load(w_out, out_buf)
+    load_up = links.load(w_up, up_buf)
     packed[seq_index] = packed_send[seq_index]
-    load_up = links.load(w_up, up_buf)
+    load_cot.wait()
+    cot_share = Share(links, cot_all, cotangent, cotangent)
+    joined_own = grad_packed.at[:, width:]
+    relative(joined_block, joined_own, 256)
+    joined_all[0] = joined_own[:, :width]
     relative(lambda place: second_low[:, columns(place * 128, 128)], first_own, 128)
     first_all[0] = first_own[:, : width // 2]
     joined_share = Share(links, joined_all, joined_all.at[0], joined_own.at[:, width:])
@@ -773,7 +784,6 @@
         return carried
 
     lax.fori_loop(0, hidden // 512, gated_step, 0)
-    cot_share.forward()
     arrived(mask_copies)
     arrived(packed_copies)
     key_index = lax.broadcasted_iota(jnp.int32, (1, 8 * rows), 1)
@@ -802,31 +812,35 @@
         attn_sum[here, :] = total
         attn_send[place] = total.astype(bfloat16)
 
-    base = links.used
-    links.used += 8
-
-    def attn_copy(mask):
-        target = exclusive(seq_index, mask)
-        return pltpu.make_async_remote_copy(
-            src_ref=attn_send.at[target],
-            dst_ref=attn_low.at[seq_index],
-            send_sem=send_sems.at[base + mask],
-            recv_sem=recv_sems.at[base + mask],
-            device_id=(dp_index, target),
-            device_id_type=MESH,
-        )
+    def by_frames(source, target):
+        base = links.used
+        links.used += 8
+
+        def copy_of(mask):
+            place = exclusive(seq_index, mask)
+            return pltpu.make_async_remote_copy(
+                src_ref=source.at[place],
+                dst_ref=target.at[seq_index],
+                send_sem=send_sems.at[base + mask],
+                recv_sem=recv_sems.at[base + mask],
+                device_id=(dp_index, place),
+                device_id_type=MESH,
+            )
+
+        return copy_of
+
+    attn_copy = by_frames(attn_send, attn_low)
 
     def attend_step(step, carried):
-        mask = 7 - step
+        mask = lax.rem(step + 4, jnp.int32(8))
         attend(exclusive(seq_index, mask))
         attn_copy(mask).start()
         return carried
 
-    lax.fori_loop(0, 7, attend_step, 0)
+    lax.fori_loop(0, 4, attend_step, 0)
+    lax.fori_loop(5, 8, attend_step, 0)
     attend(seq_index)
     attn_low[seq_index] = attn_send[seq_index]
-    joined_share.forward()
-    first_share.forward()
     load_out.wait()
     for mask in range(1, 8):
         attn_copy(jnp.int32(mask)).wait()
@@ -837,6 +851,9 @@
     gain_float = biases[:, 7 * width : 8 * width].astype(float32)
     second_all[0] = (normal * gain_float).astype(bfloat16)
     second_share = Share(links, second_all, second_all.at[0], second_all.at[0])
+    cot_share.forward()
+    joined_share.forward()
+    first_share.forward()
     small[8:] = jnp.zeros((8, small.shape[1]), float32)
     load_up.wait()
 
@@ -896,35 +913,19 @@
     relative(lambda place: attn_low[place], attn_own, 128)
     attn_all[0] = attn_own[:, : width // 2]
     attn_share = Share(links, attn_all, attn_all.at[0], attn_own.at[:, width // 2 :])
-
-    def down_step(step, total):
-        part = columns(step * 512, 512)
-        return total + product(gated[:, part], down_buf[part, :])
-
-    lower = lax.fori_loop(
-        0,
-        hidden // 512,
-        down_step,
-        residual_mid[...] + biases[:, 6 * width : 7 * width].astype(float32),
-    )
-    second_low[...] = lower.astype(bfloat16)
-    out_loads = [links.load(second_low, result)]
+    cot_share.wait()
     second_share.wait()
-    cot_share.wait()
-    for first in (0, 2):
+
+    def again(first):
         units, spots = [], []
         for number in (first, first + 1):
             place = flip(seq_index, RELATIVE[number])
-            units.append(columns(place * 512 + dp_index * 128, 128))
+            units.append(place * 512 + dp_index * 128)
             spots.append(lax.div(place, jnp.int32(2)))
-        weight_up = jnp.concatenate([up_buf[:, unit] for unit in units], axis=1)
-        weight_down = jnp.concatenate([down_buf[unit, :] for unit in units], axis=0)
+        weight_up = jnp.concatenate([up_buf[:, columns(unit, 128)] for unit in units], axis=1)
+        weight_down = jnp.concatenate([down_buf[columns(unit, 128), :] for unit in units], axis=0)
         bias = jnp.concatenate(
-            [
-                biases[:, columns(2 * width + flip(seq_index, RELATIVE[number]) * 512 + dp_index * 128, 128)]
-                for number in (first, first + 1)
-            ],
-            axis=1,
+            [biases[:, columns(2 * width + unit, 128)] for unit in units], axis=1
         ).astype(float32)
 
         def again_step(step, carried):
@@ -943,8 +944,6 @@
             return carried
 
         lax.fori_loop(0, 4, again_step, 0)
-    load_qkv = links.load(w_qkv, up_buf.at[:, : 3 * width])
-    load_skip = links.load(w_skip, down_buf.at[: 2 * width])
 
     def pair_place(number):
         base_pair = lax.div(seq_index, jnp.int32(2))
@@ -957,18 +956,23 @@
     down = Sum(links, gated_all, cot_all, down_sum, down_a, down_b)
     up = Sum(links, second_all, upper_all, up_sum, up_a, up_b, pair_place)
     out = Sum(links, attn_all, branch_all, out_sum, out_a, out_b)
-    qkv = Sum(links, first_all, packed_all, qkv_sum, qkv_a, qkv_b)
-    skip_in = Sum(links, joined_all, in_all, skip_sum, skip_a, skip_b)
+    query_part = Sum(links, first_all, packed_all.at[0], query_sum, query_a, query_b)
+    key_part = Sum(links, first_all, packed_all.at[1], key_sum, key_a, key_b)
+    value_part = Sum(links, first_all, packed_all.at[2], value_sum, value_a, value_b)
+    skip_part = Sum(links, joined_all, in_all, skip_sum, skip_a, skip_b)
+    again(2)
     down.begin()
-    up.begin()
     arrived(head_copies)
     links.sent_done(packed_copies)
-    back_send = packed_send
+    links.sent_done(head_copies)
+    query_send = attn_send
+    pair_send = packed_send.at[:, :, :256]
+    query_copy = by_frames(query_send, query_recv)
     shrink = 1.0 / math.sqrt(HEAD)
     key_total[...] = jnp.zeros_like(key_total)
     value_total[...] = jnp.zeros_like(value_total)
 
-    def back_step(place, carried):
+    def back(place):
         here = pl.ds(pl.multiple_of(place * rows, rows), rows)
         grad = grad_heads[place]
         query = packed[place, :, :128]
@@ -988,54 +992,93 @@
             value_total[...] += product_rows(low, grad_head)
         total = total * shrink
         cosine, sine = rotary(ends, place * rows, rows, 128)
-        back_send[place, :, :128] = (total * cosine - partner(total) * sine).astype(bfloat16)
+        query_send[place] = (total * cosine - partner(total) * sine).astype(bfloat16)
+
+    def back_step(step, carried):
+        mask = lax.rem(step + 4, jnp.int32(8))
+        back(exclusive(seq_index, mask))
+        query_copy(mask).start()
         return carried
 
-    lax.fori_loop(0, 8, back_step, 0)
+    lax.fori_loop(0, 4, back_step, 0)
+    lax.fori_loop(5, 8, back_step, 0)
+    back(seq_index)
+    query_recv[seq_index] = query_send[seq_index]
 
     def key_step(place, carried):
         here = pl.ds(pl.multiple_of(place * rows, rows), rows)
         total = key_total[here, :] * shrink
         cosine, sine = rotary(ends, place * rows, rows, 128)
-        back_send[place, :, 128:256] = (total * cosine - partner(total) * sine).astype(bfloat16)
-        back_send[place, :, 256:] = value_total[here, :].astype(bfloat16)
+        pair_send[place, :, :128] = (total * cosine - partner(total) * sine).astype(bfloat16)
+        pair_send[place, :, 128:] = value_total[here, :].astype(bfloat16)
         return carried
 
     lax.fori_loop(0, 8, key_step, 0)
-    back_copies = [
-        links.send(back_send.at[flip(seq_index, m)], back_recv.at[seq_index], 0, m)
+    pair_copies = [
+        links.send(pair_send.at[flip(seq_index, m)], pair_recv.at[seq_index], 0, m)
         for m in FAR_FIRST
     ]
-    back_recv[seq_index] = back_send[seq_index]
+    pair_recv[seq_index] = pair_send[seq_index]
+    again(0)
+    load_qkv = links.load(w_qkv, up_buf.at[:, : 3 * width])
+    up.begin()
     down.keep()
+    for mask in range(1, 8):
+        query_copy(jnp.int32(mask)).wait()
+    for share in (joined_share, attn_share):
+        links.sent_done([share.beside, share.corner])
+    for number in range(8):
+        grad_packed[:, number * 128 : (number + 1) * 128] = query_recv[number]
+    query_parts = quarters(grad_packed.at[:, :width], packed_all.at[0])
+    load_qkv.wait()
+
+    def first_step(step, total):
+        part = columns(step * 512, 512)
+        return total + product_cols(grad_packed[:, part], up_buf[:, part])
+
+    grad_first = lax.fori_loop(0, 2, first_step, jnp.zeros((rows, width), float32))
+    scale_normal, factor = norm_parts(residual[...])
+    attn_share.forward()
     up.keep()
-    attn_share.forward()
+    down.second()
     arrived(branch_copies)
     attn_share.wait()
     out.begin()
     out.keep()
-    arrived(back_copies)
-    for share in (joined_share, attn_share):
-        links.sent_done([share.beside, share.corner])
+
+    def down_step(step, total):
+        part = columns(step * 512, 512)
+        return total + product(gated[:, part], down_buf[part, :])
+
+    lower = lax.fori_loop(
+        0,
+        hidden // 512,
+        down_step,
+        residual_mid[...] + biases[:, 6 * width : 7 * width].astype(float32),
+    )
+    second_low[...] = lower.astype(bfloat16)
+    out_loads = [links.load(second_low, result)]
+    load_skip = links.load(w_skip, down_buf.at[: 2 * width])
+    arrived(pair_copies)
     for number in range(8):
-        for kind in range(3):
+        for kind in (1, 2):
             grad_packed[:, kind * width + number * 128 : kind * width + (number + 1) * 128] = (
-                back_recv[number, :, kind * 128 : (kind + 1) * 128]
+                pair_recv[number, :, (kind - 1) * 128 : kind * 128]
             )
-    packed_copies = quarters(grad_packed, packed_all)
-    load_qkv.wait()
-
-    def first_step(step, total):
-        part = columns(step * 512, 512)
-        return total + product_cols(grad_packed[:, part], up_buf[:, part])
-
-    grad_first = lax.fori_loop(0, 6, first_step, jnp.zeros((rows, width), float32))
-    normal, factor = norm_parts(residual[...])
+    key_parts = quarters(grad_packed.at[:, width : 2 * width], packed_all.at[1])
+    grad_first = lax.fori_loop(2, 6, first_step, grad_first)
     grad_in[...] = (
-        grad_mid[...] + norm_back(grad_first * (1.0 + scale[...]), normal, factor)
+        grad_mid[...] + norm_back(grad_first * (1.0 + scale[...]), scale_normal, factor)
     ).astype(bfloat16)
     in_copies = quarters(grad_in, in_all)
-    scaled = grad_first * normal
+    value_parts = quarters(grad_packed.at[:, 2 * width :], packed_all.at[2])
+    up.second()
+    out.second()
+    first_share.wait()
+    arrived(query_parts)
+    query_part.begin()
+    query_part.keep()
+    scaled = grad_first * scale_normal
     for number in range(len(ends)):
         member = own_segment == number
         small[number : number + 1, :width] = jnp.sum(
@@ -1054,61 +1097,65 @@
         small[...] = small_send[number].astype(float32) + small_recv[number].astype(float32)
 
     small_copy = small_start(0, 1)
-    down.second()
-    up.second()
-    first_share.wait()
-    arrived(packed_copies)
-    qkv.begin()
+    by_rows = lambda target, size: lambda index: target.at[pl.ds(index * size, size), :]
+    by_cols = lambda start, target: lambda index: target.at[:, columns(start + index * 256, 256)]
+    down.third()
+    down.gather(down.ready, by_rows(sum_down, 128))
+    arrived(key_parts)
+    key_part.begin()
+    key_part.keep()
     joined_share.wait()
     arrived(in_copies)
-    skip_in.begin()
+    skip_part.begin()
+    skip_part.keep()
+    arrived(value_parts)
+    value_part.begin()
+    value_part.keep()
     small_add(small_copy, 0)
     small_copy = small_start(1, 2)
-    out.second()
-    qkv.keep()
-    skip_in.keep()
+    query_part.second()
+    up.third()
+    up_ready[odd] = up.ready[pl.ds(pl.multiple_of(odd * 128, 128), 128), :]
+    up_other = links.send(
+        up.ready.at[pl.ds(pl.multiple_of((1 - odd) * 128, 128), 128), :], up_ready.at[odd], 0, 1
+    )
+    out.third()
+    out.gather(out.ready, by_cols(0, sum_out))
+    down.spread()
     load_skip.wait()
     for held, target, start in ((residual, grad_frames, 0), (normal_mid, grad_skip, width)):
         held[...] = product_cols(grad_in[...], down_buf[start : start + width, :])
         out_loads.append(links.load(held, target))
-    by_rows = lambda target, size: lambda index: target.at[pl.ds(index * size, size), :]
-    by_cols = lambda target, size: lambda index: target.at[:, columns(index * size, size)]
-    down.third()
-    down.gather(down.ready, by_rows(sum_down, 128))
-    up.third()
-    up_ready[odd] = up.ready[pl.ds(pl.multiple_of(odd * 128, 128), 128), :]
-    up_other = links.send(
-        up.ready.at[pl.ds(pl.multiple_of((1 - odd) * 128, 128), 128), :], up_ready.at[odd], 0, 1
-    )
+    key_part.second()
+    skip_part.second()
+    value_part.second()
     small_add(small_copy, 1)
     small_copy = small_start(2, 6)
-    out.third()
-    out.gather(out.ready, by_cols(sum_out, 256))
     up_other.wait_recv()
     up.gather(up_ready, lambda index: sum_up.at[index])
-    qkv.second()
-    skip_in.second()
+    out.spread()
+    query_part.third()
+    query_part.gather(query_part.ready, by_cols(0, sum_qkv))
+    key_part.third()
+    key_part.gather(key_part.ready, by_cols(width, sum_qkv))
+    skip_part.third()
+    skip_part.gather(skip_part.ready, by_cols(0, sum_skip))
+    value_part.third()
+    value_part.gather(value_part.ready, by_cols(2 * width, sum_qkv))
     small_add(small_copy, 2)
     small_send[3] = small[...].astype(bfloat16)
     small_copies = [
         links.send(small_send.at[3], small_all.at[dp_index], m, 0) for m in (3, 2, 1)
     ]
     small_load = links.load(small_send.at[3], small_all.at[dp_index])
-    down.spread()
-    out.spread()
-    up.spread()
-    qkv.third()
-    qkv.gather(qkv.ready, by_cols(sum_qkv, 768))
-    skip_in.third()
-    skip_in.gather(skip_in.ready, by_cols(sum_skip, 256))
-    qkv.spread()
-    skip_in.spread()
+    for each in (up, query_part, key_part, skip_part, value_part):
+        each.spread()
     small_load.wait()
     embed_load.wait()
     for load in out_loads:
         load.wait()
     arrived(small_copies + embed_copies)
-    for each in (down, up, out, qkv, skip_in):
+    for each in (down, up, out, query_part, key_part, skip_part, value_part):
         each.finish()
     links.drain()
 
@@ -1203,7 +1250,7 @@
     low = lambda *size: pltpu.VMEM(size, bfloat16)
     full = lambda *size: pltpu.VMEM(size, float32)
     biases = jnp.concatenate([b_ada, b_up, b_down, norm_gain])[None]
-    sums = ((512, 1024), (1024, 512), (512, 256), (512, 768), (1024, 256))
+    sums = ((512, 1024), (1024, 512), (512, 256), (1024, 256), (512, 256), (512, 256), (512, 256))
     sum_scratch = [low(tall // part, wide) for tall, wide in sums for part in (1, 2, 4)]
     outs = (
         (shape((rows, width), bfloat16), anywhere),
@@ -1220,22 +1267,23 @@
     parts = pl.pallas_call(
         layer_kernel,
         out_shape=tuple(item[0] for item in outs),
-        in_specs=[smem, smem] + [vmem] * 5 + [anywhere] * 6,
+        in_specs=[smem, smem] + [anywhere] * 11,
         out_specs=tuple(item[1] for item in outs),
         scratch_shapes=[
             low(*w_out.shape), low(*w_up.shape), low(*w_down.shape), low(8 * rows, 2 * width),
             low(8, rows, width), low(8, rows, width), low(8, rows, width // 2), low(8, rows, width // 2),
             low(8, rows, width), low(8, rows, 512), low(8, rows, 512), low(8, rows, 256),
-            low(8, rows, 768), low(8, rows, 256),
+            low(3, 8, rows, 256), low(8, rows, 256),
+            low(rows, width), low(rows, width), pltpu.VMEM((1, rows), jnp.int32), low(1, 8 * width),
             low(rows, width), low(16, width), pltpu.VMEM((8, 8, rows), jnp.int32),
             full(16, 2 * width), low(8, rows, 384), low(8, rows, 384), low(8, rows, 128), low(8, rows, 128),
             full(8 * rows, 128), full(rows, width), full(rows, width), full(rows, hidden), low(rows, width),
             low(rows, hidden), low(rows, hidden), full(rows, width), full(rows, width),
-            full(rows, width), low(rows, width), low(8, rows, 128), low(8, rows, 384), low(rows, 3 * width), low(rows, width), full(8 * rows, 128),
+            full(rows, width), low(rows, width), low(8, rows, 128), low(8, rows, 128), low(8, rows, 256), low(rows, 3 * width), low(rows, width), full(8 * rows, 128),
             full(8 * rows, 128), full(16, 2 * width), low(4, 16, 2 * width), low(3, 16, 2 * width),
             low(2, rows, 512),
             *sum_scratch,
-            dma((128,)), dma((128,)), dma((24,)),
+            dma((192,)), dma((192,)), dma((40,)),
         ],
         compiler_params=pltpu.CompilerParams(
             collective_id=0, has_side_effects=True, vmem_limit_bytes=60 * MIB
@@ -1266,10 +1314,10 @@
     widened = pl.pallas_call(
         widen_kernel,
         out_shape=tuple(item[0] for item in last_outs),
-        in_specs=[pl.BlockSpec(memory_space=pltpu.HBM)] * len(outs),
+        in_specs=[anywhere] * len(outs),
         out_specs=tuple(item[1] for item in last_outs),
         scratch_shapes=[*scratch, dma((10,)), dma((12,))],
-        compiler_params=pltpu.CompilerParams(vmem_limit_bytes=40 * MIB),
+        compiler_params=pltpu.CompilerParams(vmem_limit_bytes=60 * MIB),
         name="widen",
     )(*parts)
     return tuple(

time: 191 us -> 176 us (0.921)
  the two profiles are of different devices: /device:TPU:0 before, /device:TPU:26 now
where the time goes in v3:
time: 176 us
  Pallas kernels  173 us (98%)
    pallas_call x1, Pallas kernels, one_kernel(): pl.pallas_call(layer_kernel, out_shape=tuple((item[0] for item in outs)),...  167 us
    pallas_call x1, Pallas kernels, one_kernel(): pl.pallas_call(widen_kernel, out_shape=tuple((item[0] for item in last_ou...  5.97 us

profile of v3, /device:TPU:26, one launch (start us, length us, event | category | flops | bytes accessed | tf_op | source)
XLA Modules:
  0.0 175.5 jit_solution(8529529192297498103)
XLA Ops:
  0.6 0.7 pad_maximum_fusion
  1.4 0.6 broadcast_in_dim.12.bias_in
  2.0 167.4 %layer.1 = (bf16[128,1024]{1,0:T(8,128)(2,1)}, f32[128,1024]{1,0:T(8,128)}, f32[128,1024]{1,0:T(8,128)}, bf16[256,1024]{1,0:T(8,128)(2,1)}, bf16[128,3072]{1,0:T...) custom-call(s32[1,8]{1,0:T(1,128)} %lengths.1, ...), custom_call_target="tpu_custom_call" | custom-call | tf_op jit(solution)/shard_map/layer/pallas_call | solution.py:1267
  169.4 6.0 %widen.1 = (bf16[128,1024]{1,0:T(8,128)(2,1)}, f32[128,1024]{1,0:T(8,128)}, f32[128,1024]{1,0:T(8,128)}, f32[256,1024]{1,0:T(8,128)}, f32[128,2048]{1,0:T(8,128)...) custom-call(bf16[128,1024]{1,0:T(8,128)(2,1)} %get-tuple-element.36., ...), custom_call_target="tpu_custom_call" | custom-call | tf_op jit(solution)/shard_map/widen/pallas_call | solution.py:1314

commit v4 on v3

--- a/solution.py
+++ b/solution.py
@@ -669,8 +669,8 @@
     frames, skip, frame_mask, biases,
     first_own, embed_own, masks, table, packed_send, packed, attn_send, attn_low,
     attn_sum, residual, scale, grad_gated, second_low, gated, upper_parts, residual_mid, normal_mid,
-    grad_mid, branch, grad_heads, query_recv, pair_recv, grad_packed, grad_in, key_total,
-    value_total, small, small_send, small_recv, up_ready,
+    grad_mid, branch, grad_heads, query_recv, pair_recv, grad_packed, grad_in,
+    query_total, small, small_send, small_recv, up_ready,
     down_sum, down_a, down_b, up_sum, up_a, up_b, out_sum, out_a, out_b, skip_sum, skip_a, skip_b,
     query_sum, query_a, query_b, key_sum, key_a, key_b, value_sum, value_a, value_b,
     send_sems, recv_sems, load_sems,
@@ -713,11 +713,15 @@
     embed_own[...] = jnp.where(utter < steps.shape[1], embed, 0.0).astype(bfloat16)
     first_row = seq_index * rows
     cos_own, sin_own = rotary(ends, first_row, rows, 256)
+    load_mask.wait()
+    masks[0] = jnp.broadcast_to(frame_mask[...], masks.shape[1:])
+    load_cot.wait()
+    enter()
+    mask_copies = [links.send(masks.at[0], masks.at[m], 0, m) for m in range(1, 8)]
+    cot_share = Share(links, cot_all, cotangent, cotangent)
     load_frames.wait()
     load_skip_frames.wait()
-    load_mask.wait()
     load_bias.wait()
-    masks[0] = jnp.broadcast_to(frame_mask[...], masks.shape[1:])
     load_skip.wait()
     residual[...] = product(frames[...], down_buf[:width]) + product(
         skip[...], down_buf[width : 2 * width]
@@ -735,10 +739,8 @@
         spread_shift = jnp.where(member, table[number : number + 1, width:], spread_shift)
     scale[...] = spread_scale
     second_low[...] = (normal * (1.0 + spread_scale) + spread_shift).astype(bfloat16)
-    enter()
-    mask_copies = [links.send(masks.at[0], masks.at[m], 0, m) for m in range(1, 8)]
     load_qkv.wait()
-    packed_copies = []
+    packed_copies, later = [], []
     for far in (2, 1, 3, 0):
         pair = flip(lax.div(seq_index, jnp.int32(2)), far)
         parts = []
@@ -754,25 +756,24 @@
                 ]
         for mask in (2 * far, 2 * far + 1):
             if mask:
+                place = flip(seq_index, mask)
                 packed_copies.append(
                     links.send(
-                        packed_send.at[flip(seq_index, mask)], packed.at[seq_index], 0, mask
+                        packed_send.at[place, :, :256], packed.at[seq_index, :, :256], 0, mask
                     )
                 )
+                later.append((place, mask))
+    value_copies = [
+        links.send(packed_send.at[place, :, 256:], packed.at[seq_index, :, 256:], 0, mask)
+        for place, mask in later
+    ]
     load_down_low = links.load(w_down.at[: 2 * width], down_buf.at[: 2 * width])
     load_down_high = links.load(w_down.at[2 * width :], down_buf.at[2 * width :])
     load_out = links.load(w_out, out_buf)
     load_up = links.load(w_up, up_buf)
     packed[seq_index] = packed_send[seq_index]
-    load_cot.wait()
-    cot_share = Share(links, cot_all, cotangent, cotangent)
-    joined_own = grad_packed.at[:, width:]
-    relative(joined_block, joined_own, 256)
-    joined_all[0] = joined_own[:, :width]
     relative(lambda place: second_low[:, columns(place * 128, 128)], first_own, 128)
     first_all[0] = first_own[:, : width // 2]
-    joined_share = Share(links, joined_all, joined_all.at[0], joined_own.at[:, width:])
-    first_share = Share(links, first_all, first_all.at[0], first_own.at[:, width // 2 :])
     embed_copies = [links.send(embed_own, embed_all.at[dp_index], m, 0) for m in (1, 2, 3)]
     embed_load = links.load(embed_own, embed_all.at[dp_index])
     load_down_low.wait()
@@ -792,15 +793,13 @@
         [masks[exclusive(seq_index, jnp.int32(number))][:1] for number in range(8)], axis=1
     )
 
-    def attend(place):
+    def weigh(place, carried):
         query = packed[place, :, :128]
         row_index = place * rows + lax.broadcasted_iota(jnp.int32, (rows, 1), 0)
         allowed = (segments(ends, row_index) == key_segment) & (
             (key_valid > 0) | (row_index == key_index)
         )
         keys = packed[:, :, 128:256].reshape(8 * rows, 128)
-        values = packed[:, :, 256:].reshape(8 * rows, 128)
-        total = jnp.zeros((rows, 128), float32)
         here = pl.ds(pl.multiple_of(place * rows, rows), rows)
         for head in range(2):
             scores = product_cols(head_mask(query, head), keys) * (1.0 / math.sqrt(HEAD))
@@ -808,6 +807,14 @@
             raised = jnp.exp(scores - jnp.max(scores, axis=1, keepdims=True))
             low = (raised / jnp.sum(raised, axis=1, keepdims=True)).astype(bfloat16)
             weight_buf[here, head * 1024 : (head + 1) * 1024] = low
+        return carried
+
+    def attend(place):
+        values = packed[:, :, 256:].reshape(8 * rows, 128)
+        total = jnp.zeros((rows, 128), float32)
+        here = pl.ds(pl.multiple_of(place * rows, rows), rows)
+        for head in range(2):
+            low = weight_buf[here, head * 1024 : (head + 1) * 1024]
             total = total + product(low, head_mask(values, head))
         attn_sum[here, :] = total
         attn_send[place] = total.astype(bfloat16)
@@ -837,6 +844,8 @@
         attn_copy(mask).start()
         return carried
 
+    lax.fori_loop(0, 8, weigh, 0)
+    arrived(value_copies)
     lax.fori_loop(0, 4, attend_step, 0)
     lax.fori_loop(5, 8, attend_step, 0)
     attend(seq_index)
@@ -852,8 +861,6 @@
     second_all[0] = (normal * gain_float).astype(bfloat16)
     second_share = Share(links, second_all, second_all.at[0], second_all.at[0])
     cot_share.forward()
-    joined_share.forward()
-    first_share.forward()
     small[8:] = jnp.zeros((8, small.shape[1]), float32)
     load_up.wait()
 
@@ -909,11 +916,22 @@
 
     second_share.forward()
     branch_copies = quarters(branch, branch_all)
-    attn_own = grad_packed.at[:, :width]
+    attn_own = upper_parts.at[:, 2 * width : 3 * width]
     relative(lambda place: attn_low[place], attn_own, 128)
     attn_all[0] = attn_own[:, : width // 2]
     attn_share = Share(links, attn_all, attn_all.at[0], attn_own.at[:, width // 2 :])
     cot_share.wait()
+    joined_own = upper_parts.at[:, : 2 * width]
+    relative(joined_block, joined_own, 256)
+    joined_all[0] = joined_own[:, :width]
+
+    def table_step(place, carried):
+        cosine, sine = rotary(ends, place * rows, rows, 128)
+        grad_gated[:, columns(place * 512, 128)] = cosine
+        grad_gated[:, columns(place * 512 + 128, 128)] = sine
+        return carried
+
+    lax.fori_loop(0, 8, table_step, 0)
     second_share.wait()
 
     def again(first):
@@ -963,121 +981,151 @@
     again(2)
     down.begin()
     arrived(head_copies)
-    links.sent_done(packed_copies)
+    links.sent_done(packed_copies + value_copies)
     links.sent_done(head_copies)
     query_send = attn_send
     pair_send = packed_send.at[:, :, :256]
-    query_copy = by_frames(query_send, query_recv)
+    first_share = Share(links, first_all, first_all.at[0], first_own.at[:, width // 2 :])
+    pair_copy = by_frames(pair_send, pair_recv)
     shrink = 1.0 / math.sqrt(HEAD)
-    key_total[...] = jnp.zeros_like(key_total)
-    value_total[...] = jnp.zeros_like(value_total)
-
-    def back(place):
+    query_total[...] = jnp.zeros_like(query_total)
+
+    def delta_step(place, carried):
         here = pl.ds(pl.multiple_of(place * rows, rows), rows)
-        grad = grad_heads[place]
-        query = packed[place, :, :128]
-        keys = packed[:, :, 128:256].reshape(8 * rows, 128)
-        values = packed[:, :, 256:].reshape(8 * rows, 128)
-        both = grad.astype(float32) * attn_sum[here, :]
-        total = jnp.zeros((rows, 128), float32)
+        both = grad_heads[place].astype(float32) * attn_sum[here, :]
         for head in range(2):
-            low = weight_buf[here, head * 1024 : (head + 1) * 1024]
+            delta = jnp.sum(head_mask(both, head), axis=1, keepdims=True)
+            grad_gated[:, columns(place * 512 + 256 + head * 128, 128)] = jnp.broadcast_to(
+                delta, (rows, 128)
+            )
+        return carried
+
+    lax.fori_loop(0, 8, delta_step, 0)
+
+    def turned_back(total, place):
+        cosine = grad_gated[:, columns(place * 512, 128)]
+        sine = grad_gated[:, columns(place * 512 + 128, 128)]
+        total = total * shrink
+        return (total * cosine - partner(total) * sine).astype(bfloat16)
+
+    def back(pair):
+        both = pl.ds(2 * pair, 2)
+        keys = packed[both, :, 128:256].reshape(2 * rows, 128)
+        values = packed[both, :, 256:].reshape(2 * rows, 128)
+        queries = packed[:, :, :128].reshape(8 * rows, 128)
+        grad = grad_heads[...].reshape(8 * rows, 128)
+        grad_keys = jnp.zeros((2 * rows, 128), float32)
+        grad_values = jnp.zeros((2 * rows, 128), float32)
+        for head in range(2):
+            low = weight_buf[:, columns(head * 1024 + pair * 256, 256)]
             grad_head = head_mask(grad, head)
-            delta = jnp.sum(head_mask(both, head), axis=1, keepdims=True)
+            delta = jnp.concatenate(
+                [
+                    grad_gated[:, place * 512 + 256 + head * 128 : place * 512 + 384 + head * 128]
+                    for place in range(8)
+                ],
+                axis=0,
+            )
+            delta = jnp.concatenate([delta, delta], axis=1)
             grad_scores = (
                 low.astype(float32) * (product_cols(grad_head, values) - delta)
             ).astype(bfloat16)
-            total = total + product(grad_scores, head_mask(keys, head))
-            key_total[...] += product_rows(grad_scores, head_mask(query, head))
-            value_total[...] += product_rows(low, grad_head)
-        total = total * shrink
-        cosine, sine = rotary(ends, place * rows, rows, 128)
-        query_send[place] = (total * cosine - partner(total) * sine).astype(bfloat16)
+            query_total[...] += product(grad_scores, head_mask(keys, head))
+            grad_keys = grad_keys + product_rows(grad_scores, head_mask(queries, head))
+            grad_values = grad_values + product_rows(low, grad_head)
+        for side in range(2):
+            place = 2 * pair + side
+            part = slice(side * rows, (side + 1) * rows)
+            pair_send[place, :, :128] = turned_back(grad_keys[part], place)
+            pair_send[place, :, 128:] = grad_values[part].astype(bfloat16)
+
+    own_pair = lax.div(seq_index, jnp.int32(2))
 
     def back_step(step, carried):
-        mask = lax.rem(step + 4, jnp.int32(8))
-        back(exclusive(seq_index, mask))
-        query_copy(mask).start()
+        far = step + 2 - 3 * lax.div(step, jnp.int32(2))
+        back(lax.div(exclusive(seq_index, 2 * far), jnp.int32(2)))
+        pair_copy(2 * far).start()
+        pair_copy(2 * far + 1).start()
         return carried
 
-    lax.fori_loop(0, 4, back_step, 0)
-    lax.fori_loop(5, 8, back_step, 0)
-    back(seq_index)
-    query_recv[seq_index] = query_send[seq_index]
-
-    def key_step(place, carried):
+    lax.fori_loop(0, 3, back_step, 0)
+    back(own_pair)
+    pair_copy(jnp.int32(1)).start()
+    pair_recv[seq_index] = pair_send[seq_index]
+
+    def query_step(place, carried):
         here = pl.ds(pl.multiple_of(place * rows, rows), rows)
-        total = key_total[here, :] * shrink
-        cosine, sine = rotary(ends, place * rows, rows, 128)
-        pair_send[place, :, :128] = (total * cosine - partner(total) * sine).astype(bfloat16)
-        pair_send[place, :, 128:] = value_total[here, :].astype(bfloat16)
+        query_send[place] = turned_back(query_total[here, :], place)
         return carried
 
-    lax.fori_loop(0, 8, key_step, 0)
-    pair_copies = [
-        links.send(pair_send.at[flip(seq_index, m)], pair_recv.at[seq_index], 0, m)
+    lax.fori_loop(0, 8, query_step, 0)
+    query_copies = [
+        links.send(query_send.at[flip(seq_index, m)], query_recv.at[seq_index], 0, m)
         for m in FAR_FIRST
     ]
-    pair_recv[seq_index] = pair_send[seq_index]
+    query_recv[seq_index] = query_send[seq_index]
     again(0)
     load_qkv = links.load(w_qkv, up_buf.at[:, : 3 * width])
     up.begin()
     down.keep()
+
+    def down_step(step, total):
+        part = columns(step * 512, 512)
+        return total + product(gated[:, part], down_buf[part, :])
+
+    lower = lax.fori_loop(
+        0,
+        hidden // 512,
+        down_step,
+        residual_mid[...] + biases[:, 6 * width : 7 * width].astype(float32),
+    )
+    second_low[...] = lower.astype(bfloat16)
+    out_loads = [links.load(second_low, result)]
+    load_skip = links.load(w_skip, down_buf.at[: 2 * width])
     for mask in range(1, 8):
-        query_copy(jnp.int32(mask)).wait()
-    for share in (joined_share, attn_share):
-        links.sent_done([share.beside, share.corner])
+        pair_copy(jnp.int32(mask)).wait()
+    for number in range(8):
+        for kind in (1, 2):
+            grad_packed[:, kind * width + number * 128 : kind * width + (number + 1) * 128] = (
+                pair_recv[number, :, (kind - 1) * 128 : kind * 128]
+            )
+    key_parts = quarters(grad_packed.at[:, width : 2 * width], packed_all.at[1])
+    value_parts = quarters(grad_packed.at[:, 2 * width :], packed_all.at[2])
+    joined_share = Share(links, joined_all, joined_all.at[0], joined_own.at[:, width:])
+    load_qkv.wait()
+
+    def first_step(step, total):
+        part = columns(step * 512, 512)
+        return total + product_cols(grad_packed[:, part], up_buf[:, part])
+
+    grad_first = lax.fori_loop(2, 6, first_step, jnp.zeros((rows, width), float32))
+    scale_normal, factor = norm_parts(residual[...])
+    arrived(query_copies)
     for number in range(8):
         grad_packed[:, number * 128 : (number + 1) * 128] = query_recv[number]
     query_parts = quarters(grad_packed.at[:, :width], packed_all.at[0])
-    load_qkv.wait()
-
-    def first_step(step, total):
-        part = columns(step * 512, 512)
-        return total + product_cols(grad_packed[:, part], up_buf[:, part])
-
-    grad_first = lax.fori_loop(0, 2, first_step, jnp.zeros((rows, width), float32))
-    scale_normal, factor = norm_parts(residual[...])
+    grad_first = lax.fori_loop(0, 2, first_step, grad_first)
+    grad_in[...] = (
+        grad_mid[...] + norm_back(grad_first * (1.0 + scale[...]), scale_normal, factor)
+    ).astype(bfloat16)
+    in_copies = quarters(grad_in, in_all)
     attn_share.forward()
+    first_share.forward()
     up.keep()
     down.second()
     arrived(branch_copies)
     attn_share.wait()
     out.begin()
     out.keep()
-
-    def down_step(step, total):
-        part = columns(step * 512, 512)
-        return total + product(gated[:, part], down_buf[part, :])
-
-    lower = lax.fori_loop(
-        0,
-        hidden // 512,
-        down_step,
-        residual_mid[...] + biases[:, 6 * width : 7 * width].astype(float32),
-    )
-    second_low[...] = lower.astype(bfloat16)
-    out_loads = [links.load(second_low, result)]
-    load_skip = links.load(w_skip, down_buf.at[: 2 * width])
-    arrived(pair_copies)
-    for number in range(8):
-        for kind in (1, 2):
-            grad_packed[:, kind * width + number * 128 : kind * width + (number + 1) * 128] = (
-                pair_recv[number, :, (kind - 1) * 128 : kind * 128]
-            )
-    key_parts = quarters(grad_packed.at[:, width : 2 * width], packed_all.at[1])
-    grad_first = lax.fori_loop(2, 6, first_step, grad_first)
-    grad_in[...] = (
-        grad_mid[...] + norm_back(grad_first * (1.0 + scale[...]), scale_normal, factor)
-    ).astype(bfloat16)
-    in_copies = quarters(grad_in, in_all)
-    value_parts = quarters(grad_packed.at[:, 2 * width :], packed_all.at[2])
     up.second()
+    first_share.wait()
+    arrived(key_parts)
+    key_part.begin()
+    key_part.keep()
+    arrived(value_parts)
+    value_part.begin()
+    value_part.keep()
     out.second()
-    first_share.wait()
-    arrived(query_parts)
-    query_part.begin()
-    query_part.keep()
     scaled = grad_first * scale_normal
     for number in range(len(ends)):
         member = own_segment == number
@@ -1101,19 +1149,18 @@
     by_cols = lambda start, target: lambda index: target.at[:, columns(start + index * 256, 256)]
     down.third()
     down.gather(down.ready, by_rows(sum_down, 128))
-    arrived(key_parts)
-    key_part.begin()
-    key_part.keep()
+    arrived(query_parts)
+    query_part.begin()
+    query_part.keep()
+    key_part.second()
+    joined_share.forward()
     joined_share.wait()
     arrived(in_copies)
     skip_part.begin()
     skip_part.keep()
-    arrived(value_parts)
-    value_part.begin()
-    value_part.keep()
+    value_part.second()
     small_add(small_copy, 0)
     small_copy = small_start(1, 2)
-    query_part.second()
     up.third()
     up_ready[odd] = up.ready[pl.ds(pl.multiple_of(odd * 128, 128), 128), :]
     up_other = links.send(
@@ -1126,29 +1173,28 @@
     for held, target, start in ((residual, grad_frames, 0), (normal_mid, grad_skip, width)):
         held[...] = product_cols(grad_in[...], down_buf[start : start + width, :])
         out_loads.append(links.load(held, target))
-    key_part.second()
+    query_part.second()
     skip_part.second()
-    value_part.second()
     small_add(small_copy, 1)
     small_copy = small_start(2, 6)
     up_other.wait_recv()
     up.gather(up_ready, lambda index: sum_up.at[index])
     out.spread()
+    key_part.third()
+    key_part.gather(key_part.ready, by_cols(width, sum_qkv))
+    value_part.third()
+    value_part.gather(value_part.ready, by_cols(2 * width, sum_qkv))
     query_part.third()
     query_part.gather(query_part.ready, by_cols(0, sum_qkv))
-    key_part.third()
-    key_part.gather(key_part.ready, by_cols(width, sum_qkv))
     skip_part.third()
     skip_part.gather(skip_part.ready, by_cols(0, sum_skip))
-    value_part.third()
-    value_part.gather(value_part.ready, by_cols(2 * width, sum_qkv))
     small_add(small_copy, 2)
     small_send[3] = small[...].astype(bfloat16)
     small_copies = [
         links.send(small_send.at[3], small_all.at[dp_index], m, 0) for m in (3, 2, 1)
     ]
     small_load = links.load(small_send.at[3], small_all.at[dp_index])
-    for each in (up, query_part, key_part, skip_part, value_part):
+    for each in (up, key_part, value_part, query_part, skip_part):
         each.spread()
     small_load.wait()
     embed_load.wait()
@@ -1280,10 +1326,10 @@
             full(8 * rows, 128), full(rows, width), full(rows, width), full(rows, hidden), low(rows, width),
             low(rows, hidden), low(rows, hidden), full(rows, width), full(rows, width),
             full(rows, width), low(rows, width), low(8, rows, 128), low(8, rows, 128), low(8, rows, 256), low(rows, 3 * width), low(rows, width), full(8 * rows, 128),
-            full(8 * rows, 128), full(16, 2 * width), low(4, 16, 2 * width), low(3, 16, 2 * width),
+            full(16, 2 * width), low(4, 16, 2 * width), low(3, 16, 2 * width),
             low(2, rows, 512),
             *sum_scratch,
-            dma((192,)), dma((192,)), dma((40,)),
+            dma((168,)), dma((168,)), dma((28,)),
         ],
         compiler_params=pltpu.CompilerParams(
             collective_id=0, has_side_effects=True, vmem_limit_bytes=60 * MIB

time: 176 us -> 162 us (0.920)
  the two profiles are of different devices: /device:TPU:26 before, /device:TPU:0 now
where the time goes in v4:
time: 162 us; the launch traced here: 161 us
  Pallas kernels  159 us (98%)
    pallas_call x1, Pallas kernels, one_kernel(): pl.pallas_call(layer_kernel, out_shape=tuple((item[0] for item in outs)),...  153 us
    pallas_call x1, Pallas kernels, one_kernel(): pl.pallas_call(widen_kernel, out_shape=tuple((item[0] for item in last_ou...  5.97 us

profile of v4, /device:TPU:0, one launch (start us, length us, event | category | flops | bytes accessed | tf_op | source)
XLA Modules:
  0.0 160.8 jit_solution(6100550335242071881)
XLA Ops:
  0.6 0.7 pad_maximum_fusion
  1.4 0.6 broadcast_in_dim.12.bias_in
  2.0 152.6 %layer.1 = (bf16[128,1024]{1,0:T(8,128)(2,1)}, f32[128,1024]{1,0:T(8,128)}, f32[128,1024]{1,0:T(8,128)}, bf16[256,1024]{1,0:T(8,128)(2,1)}, bf16[128,3072]{1,0:T...) custom-call(s32[1,8]{1,0:T(1,128)} %lengths.1, ...), custom_call_target="tpu_custom_call" | custom-call | tf_op jit(solution)/shard_map/layer/pallas_call | solution.py:1313
  154.6 6.0 %widen.1 = (bf16[128,1024]{1,0:T(8,128)(2,1)}, f32[128,1024]{1,0:T(8,128)}, f32[128,1024]{1,0:T(8,128)}, f32[256,1024]{1,0:T(8,128)}, f32[128,2048]{1,0:T(8,128)...) custom-call(bf16[128,1024]{1,0:T(8,128)(2,1)} %get-tuple-element.36., ...), custom_call_target="tpu_custom_call" | custom-call | tf_op jit(solution)/shard_map/widen/pallas_call | solution.py:1360

commit v5 on v4

--- a/solution.py
+++ b/solution.py
@@ -598,26 +598,46 @@
 
 
 class Sum:
-    def __init__(self, links, left, right, total, into_a, into_b, place=None):
+    def __init__(
+        self, links, left, right, total, into_a, into_b, place=None, beside=None
+    ):
         self.links, self.left, self.right, self.total = links, left, right, total
-        self.into_a, self.into_b, self.place = into_a, into_b, place
+        self.into_a, self.into_b, self.place, self.beside = into_a, into_b, place, beside
         self.size = total.shape[0] // 4
 
+    def piece(self, source):
+        depth = self.left.shape[0] * self.left.shape[1]
+        return product_rows(
+            self.left[:, :, columns(source, 256)].reshape(depth, 256),
+            self.right[...].reshape(depth, self.right.shape[2]),
+        )
+
     def fill(self, low, high):
-        depth = self.left.shape[0] * self.left.shape[1]
-
         def step(number, carried):
             start = pl.multiple_of(number * 256, 256)
             source = start if self.place is None else self.place(number)
-            self.total[pl.ds(start, 256), :] = product_rows(
-                self.left[:, :, columns(source, 256)].reshape(depth, 256),
-                self.right[...].reshape(depth, self.right.shape[2]),
-            ).astype(jnp.bfloat16)
+            made = self.piece(source)
+            if self.beside is not None:
+                made = made + self.beside[1][pl.ds(start, 256), :].astype(jnp.float32)
+            self.total[pl.ds(start, 256), :] = made.astype(jnp.bfloat16)
             return carried
 
         lax.fori_loop(low // 256, high // 256, step, 0)
 
+    def begin_beside(self):
+        out, into = self.beside
+
+        def step(number, carried):
+            start = pl.multiple_of(number * 256, 256)
+            out[pl.ds(start, 256), :] = self.piece(4 * self.size + start).astype(jnp.bfloat16)
+            return carried
+
+        lax.fori_loop(0, 4 * self.size // 256, step, 0)
+        self.beside_copy = self.links.send(out, into, 0, 1)
+
     def begin(self):
+        if self.beside is not None:
+            self.beside_copy.wait_recv()
         self.fill(2 * self.size, 4 * self.size)
         self.copy = self.links.send(self.total.at[2 * self.size :], self.into_a, 0, 2)
 
@@ -670,8 +690,8 @@
     first_own, embed_own, masks, table, packed_send, packed, attn_send, attn_low,
     attn_sum, residual, scale, grad_gated, second_low, gated, upper_parts, residual_mid, normal_mid,
     grad_mid, branch, grad_heads, query_recv, pair_recv, grad_packed, grad_in,
-    query_total, small, small_send, small_recv, up_ready,
-    down_sum, down_a, down_b, up_sum, up_a, up_b, out_sum, out_a, out_b, skip_sum, skip_a, skip_b,
+    query_total, turns, small, small_send, small_recv, up_ready,
+    down_sum, down_a, down_b, up_sum, up_a, up_b, out_sum, out_a, out_b, skip_sum, skip_a, skip_b, skip_out, skip_beside,
     query_sum, query_a, query_b, key_sum, key_a, key_b, value_sum, value_a, value_b,
     send_sems, recv_sems, load_sems,
 ):
@@ -713,14 +733,17 @@
     embed_own[...] = jnp.where(utter < steps.shape[1], embed, 0.0).astype(bfloat16)
     first_row = seq_index * rows
     cos_own, sin_own = rotary(ends, first_row, rows, 256)
+    load_frames.wait()
+    load_skip_frames.wait()
+    relative(joined_block, joined_all.at[0], 256)
     load_mask.wait()
     masks[0] = jnp.broadcast_to(frame_mask[...], masks.shape[1:])
     load_cot.wait()
     enter()
     mask_copies = [links.send(masks.at[0], masks.at[m], 0, m) for m in range(1, 8)]
     cot_share = Share(links, cot_all, cotangent, cotangent)
-    load_frames.wait()
-    load_skip_frames.wait()
+    joined_across = links.send(joined_all.at[0], joined_all.at[2], 2, 0)
+    joined_core = links.send(joined_all.at[0], joined_all.at[1], 1, 0)
     load_bias.wait()
     load_skip.wait()
     residual[...] = product(frames[...], down_buf[:width]) + product(
@@ -785,6 +808,15 @@
         return carried
 
     lax.fori_loop(0, hidden // 512, gated_step, 0)
+
+    def table_step(place, carried):
+        here = pl.ds(pl.multiple_of(place * rows, rows), rows)
+        cosine, sine = rotary(ends, place * rows, rows, 128)
+        turns[here, :128] = cosine
+        turns[here, 128:] = sine
+        return carried
+
+    lax.fori_loop(0, 8, table_step, 0)
     arrived(mask_copies)
     arrived(packed_copies)
     key_index = lax.broadcasted_iota(jnp.int32, (1, 8 * rows), 1)
@@ -904,14 +936,14 @@
     ]
     grad_heads[seq_index] = grad_send[seq_index]
 
-    def quarters(source, slots):
+    def quarters(source, slots, group=GROUP):
         size = slots.shape[2]
         slots[0] = source[:, columns(dp_index * size, size)]
         return [
             links.send(
                 source.at[:, columns(flip(dp_index, m) * size, size)], slots.at[4 * v + m], m, v
             )
-            for m, v in GROUP
+            for m, v in group
         ]
 
     second_share.forward()
@@ -921,17 +953,8 @@
     attn_all[0] = attn_own[:, : width // 2]
     attn_share = Share(links, attn_all, attn_all.at[0], attn_own.at[:, width // 2 :])
     cot_share.wait()
-    joined_own = upper_parts.at[:, : 2 * width]
-    relative(joined_block, joined_own, 256)
-    joined_all[0] = joined_own[:, :width]
-
-    def table_step(place, carried):
-        cosine, sine = rotary(ends, place * rows, rows, 128)
-        grad_gated[:, columns(place * 512, 128)] = cosine
-        grad_gated[:, columns(place * 512 + 128, 128)] = sine
-        return carried
-
-    lax.fori_loop(0, 8, table_step, 0)
+    joined_across.wait_recv()
+    joined_far = links.send(joined_all.at[2], joined_all.at[3], 1, 0)
     second_share.wait()
 
     def again(first):
@@ -977,7 +1000,9 @@
     query_part = Sum(links, first_all, packed_all.at[0], query_sum, query_a, query_b)
     key_part = Sum(links, first_all, packed_all.at[1], key_sum, key_a, key_b)
     value_part = Sum(links, first_all, packed_all.at[2], value_sum, value_a, value_b)
-    skip_part = Sum(links, joined_all, in_all, skip_sum, skip_a, skip_b)
+    skip_part = Sum(
+        links, joined_all, in_all, skip_sum, skip_a, skip_b, beside=(skip_out, skip_beside)
+    )
     again(2)
     down.begin()
     arrived(head_copies)
@@ -1003,8 +1028,8 @@
     lax.fori_loop(0, 8, delta_step, 0)
 
     def turned_back(total, place):
-        cosine = grad_gated[:, columns(place * 512, 128)]
-        sine = grad_gated[:, columns(place * 512 + 128, 128)]
+        here = pl.ds(pl.multiple_of(place * rows, rows), rows)
+        cosine, sine = turns[here, :128], turns[here, 128:]
         total = total * shrink
         return (total * cosine - partner(total) * sine).astype(bfloat16)
 
@@ -1091,7 +1116,6 @@
             )
     key_parts = quarters(grad_packed.at[:, width : 2 * width], packed_all.at[1])
     value_parts = quarters(grad_packed.at[:, 2 * width :], packed_all.at[2])
-    joined_share = Share(links, joined_all, joined_all.at[0], joined_own.at[:, width:])
     load_qkv.wait()
 
     def first_step(step, total):
@@ -1100,25 +1124,27 @@
 
     grad_first = lax.fori_loop(2, 6, first_step, jnp.zeros((rows, width), float32))
     scale_normal, factor = norm_parts(residual[...])
+    down.second()
     arrived(query_copies)
     for number in range(8):
         grad_packed[:, number * 128 : (number + 1) * 128] = query_recv[number]
-    query_parts = quarters(grad_packed.at[:, :width], packed_all.at[0])
     grad_first = lax.fori_loop(0, 2, first_step, grad_first)
     grad_in[...] = (
         grad_mid[...] + norm_back(grad_first * (1.0 + scale[...]), scale_normal, factor)
     ).astype(bfloat16)
-    in_copies = quarters(grad_in, in_all)
+    in_copies = quarters(grad_in, in_all, ((2, 0), (3, 0), (1, 0)))
+    query_parts = quarters(grad_packed.at[:, :width], packed_all.at[0])
     attn_share.forward()
     first_share.forward()
     up.keep()
-    down.second()
     arrived(branch_copies)
     attn_share.wait()
     out.begin()
     out.keep()
     up.second()
     first_share.wait()
+    arrived([joined_core, joined_far] + in_copies)
+    skip_part.begin_beside()
     arrived(key_parts)
     key_part.begin()
     key_part.keep()
@@ -1153,9 +1179,6 @@
     query_part.begin()
     query_part.keep()
     key_part.second()
-    joined_share.forward()
-    joined_share.wait()
-    arrived(in_copies)
     skip_part.begin()
     skip_part.keep()
     value_part.second()
@@ -1298,6 +1321,7 @@
     biases = jnp.concatenate([b_ada, b_up, b_down, norm_gain])[None]
     sums = ((512, 1024), (1024, 512), (512, 256), (1024, 256), (512, 256), (512, 256), (512, 256))
     sum_scratch = [low(tall // part, wide) for tall, wide in sums for part in (1, 2, 4)]
+    sum_scratch[12:12] = [low(1024, 256), low(1024, 256)]
     outs = (
         (shape((rows, width), bfloat16), anywhere),
         (shape((rows, width), float32), anywhere),
@@ -1317,22 +1341,22 @@
         out_specs=tuple(item[1] for item in outs),
         scratch_shapes=[
             low(*w_out.shape), low(*w_up.shape), low(*w_down.shape), low(8 * rows, 2 * width),
-            low(8, rows, width), low(8, rows, width), low(8, rows, width // 2), low(8, rows, width // 2),
+            low(4, rows, 2 * width), low(8, rows, width), low(8, rows, width // 2), low(8, rows, width // 2),
             low(8, rows, width), low(8, rows, 512), low(8, rows, 512), low(8, rows, 256),
-            low(3, 8, rows, 256), low(8, rows, 256),
+            low(3, 8, rows, 256), low(4, rows, 256),
             low(rows, width), low(rows, width), pltpu.VMEM((1, rows), jnp.int32), low(1, 8 * width),
             low(rows, width), low(16, width), pltpu.VMEM((8, 8, rows), jnp.int32),
             full(16, 2 * width), low(8, rows, 384), low(8, rows, 384), low(8, rows, 128), low(8, rows, 128),
             full(8 * rows, 128), full(rows, width), full(rows, width), full(rows, hidden), low(rows, width),
             low(rows, hidden), low(rows, hidden), full(rows, width), full(rows, width),
-            full(rows, width), low(rows, width), low(8, rows, 128), low(8, rows, 128), low(8, rows, 256), low(rows, 3 * width), low(rows, width), full(8 * rows, 128),
+            full(rows, width), low(rows, width), low(8, rows, 128), low(8, rows, 128), low(8, rows, 256), low(rows, 3 * width), low(rows, width), full(8 * rows, 128), full(8 * rows, 256),
             full(16, 2 * width), low(4, 16, 2 * width), low(3, 16, 2 * width),
             low(2, rows, 512),
             *sum_scratch,
             dma((168,)), dma((168,)), dma((28,)),
         ],
         compiler_params=pltpu.CompilerParams(
-            collective_id=0, has_side_effects=True, vmem_limit_bytes=60 * MIB
+            collective_id=0, has_side_effects=True, vmem_limit_bytes=62 * MIB
         ),
         name="layer",
     )(

time: 162 us -> 160 us (0.988)
  no operation moved by 1% of the time
where the time goes in v5:
time: 160 us
  Pallas kernels  158 us (99%)
    pallas_call x1, Pallas kernels, one_kernel(): pl.pallas_call(layer_kernel, out_shape=tuple((item[0] for item in outs)),...  152 us
    pallas_call x1, Pallas kernels, one_kernel(): pl.pallas_call(widen_kernel, out_shape=tuple((item[0] for item in last_ou...  5.97 us

profile of v5, /device:TPU:0, one launch (start us, length us, event | category | flops | bytes accessed | tf_op | source)
XLA Modules:
  0.0 159.8 jit_solution(15087731390262710566)
XLA Ops:
  0.6 0.7 pad_maximum_fusion
  1.4 0.6 broadcast_in_dim.12.bias_in
  2.0 151.6 %layer.1 = (bf16[128,1024]{1,0:T(8,128)(2,1)}, f32[128,1024]{1,0:T(8,128)}, f32[128,1024]{1,0:T(8,128)}, bf16[256,1024]{1,0:T(8,128)(2,1)}, bf16[128,3072]{1,0:T...) custom-call(s32[1,8]{1,0:T(1,128)} %lengths.1, ...), custom_call_target="tpu_custom_call" | custom-call | tf_op jit(solution)/shard_map/layer/pallas_call | solution.py:1337
  153.7 6.0 %widen.1 = (bf16[128,1024]{1,0:T(8,128)(2,1)}, f32[128,1024]{1,0:T(8,128)}, f32[128,1024]{1,0:T(8,128)}, f32[256,1024]{1,0:T(8,128)}, f32[128,2048]{1,0:T(8,128)...) custom-call(bf16[128,1024]{1,0:T(8,128)(2,1)} %get-tuple-element.36., ...), custom_call_target="tpu_custom_call" | custom-call | tf_op jit(solution)/shard_map/widen/pallas_call | solution.py:1384

commit v6 on v5

--- a/solution.py
+++ b/solution.py
@@ -1238,14 +1238,14 @@
 ):
     float32 = jnp.float32
     seq_index = lax.axis_index("seq")
-    sources = (sum_up, sum_down, sum_qkv, sum_skip, small_all, embed_all, sum_out, result_in, frames_in, skip_in)
-    inside = (low_up, low_down, low_qkv, low_w_skip, low_small, low_embed, low_out, low_result, low_frames, low_skip)
+    sources = (sum_up, sum_down, sum_qkv, sum_skip, small_all, embed_all, sum_out)
+    inside = (low_up, low_down, low_qkv, low_w_skip, low_small, low_embed, low_out)
     loads = [
         pltpu.make_async_copy(source, target, in_sems.at[number])
         for number, (source, target) in enumerate(zip(sources, inside, strict=True))
     ]
-    for load in loads:
-        load.start()
+    for number in (6, 3, 2, 1, 0, 4, 5):
+        loads[number].start()
     stores = []
 
     def store(source, target):
@@ -1253,6 +1253,17 @@
         copy.start()
         stores.append(copy)
 
+    for whole, out in ((frames_in, grad_frames), (skip_in, grad_skip), (result_in, result)):
+        store(whole, out)
+    for number, low, full, out in (
+        (6, low_out, full_out, out_out),
+        (3, low_w_skip, full_skip, out_skip),
+        (2, low_qkv, full_qkv, out_qkv),
+        (1, low_down, full_down, out_down),
+    ):
+        loads[number].wait()
+        full[...] = low[...].astype(float32)
+        store(full, out)
     loads[0].wait()
     for quarter in range(4):
         for side in range(2):
@@ -1262,26 +1273,12 @@
                     quarter, side, :, level * 128 : (level + 1) * 128
                 ].astype(float32)
     store(full_up, out_up)
-    for number, low, full, out in (
-        (1, low_down, full_down, out_down),
-        (2, low_qkv, full_qkv, out_qkv),
-        (3, low_w_skip, full_skip, out_skip),
-    ):
-        loads[number].wait()
-        full[...] = low[...].astype(float32)
-        store(full, out)
     loads[4].wait()
     loads[5].wait()
     size = full_ada.shape[0]
     own = low_embed[:, :, columns(seq_index * size, size)].reshape(-1, size)
     full_ada[...] = product_rows(own, low_small[...].reshape(own.shape[0], full_ada.shape[1]))
     store(full_ada, out_ada)
-    loads[6].wait()
-    full_out[...] = low_out[...].astype(float32)
-    store(full_out, out_out)
-    for number, low, out in ((7, low_result, result), (8, low_frames, grad_frames), (9, low_skip, grad_skip)):
-        loads[number].wait()
-        store(low, out)
     wide = low_small.shape[2]
     spot = columns(seq_index * 256, 256)
     bias = jnp.zeros((1, 256), float32)

time: 160 us -> 196 us (1.23)
  Pallas kernels: 158 us -> 193 us
    pallas_call x1, Pallas kernels: 5.97 us -> 41.6 us  [one_kernel(): pl.pallas_call(widen_kernel, out_shape=tuple((item[0] for item in last_ou...]
where the time goes in v6:
time: 196 us; the launch traced here: 195 us
  Pallas kernels  193 us (98%)
    pallas_call x1, Pallas kernels, one_kernel(): pl.pallas_call(layer_kernel, out_shape=tuple((item[0] for item in outs)),...  152 us
    pallas_call x1, Pallas kernels, one_kernel(): pl.pallas_call(widen_kernel, out_shape=tuple((item[0] for item in last_ou...  41.6 us

profile of v6, /device:TPU:0, one launch (start us, length us, event | category | flops | bytes accessed | tf_op | source)
XLA Modules:
  0.0 195.5 jit_solution(14543886181059407979)
XLA Ops:
  0.6 0.7 pad_maximum_fusion
  1.4 0.6 broadcast_in_dim.12.bias_in
  2.0 151.6 %layer.1 = (bf16[128,1024]{1,0:T(8,128)(2,1)}, f32[128,1024]{1,0:T(8,128)}, f32[128,1024]{1,0:T(8,128)}, bf16[256,1024]{1,0:T(8,128)(2,1)}, bf16[128,3072]{1,0:T...) custom-call(s32[1,8]{1,0:T(1,128)} %lengths.1, ...), custom_call_target="tpu_custom_call" | custom-call | tf_op jit(solution)/shard_map/layer/pallas_call | solution.py:1334
  153.7 41.6 %widen.1 = (bf16[128,1024]{1,0:T(8,128)(2,1)}, f32[128,1024]{1,0:T(8,128)}, f32[128,1024]{1,0:T(8,128)}, f32[256,1024]{1,0:T(8,128)}, f32[128,2048]{1,0:T(8,128)...) custom-call(bf16[128,1024]{1,0:T(8,128)(2,1)} %get-tuple-element.36., ...), custom_call_target="tpu_custom_call" | custom-call | tf_op jit(solution)/shard_map/widen/pallas_call | solution.py:1381
